TPU v7x, 512 devices: a whole 4x8x8 slice. The times are simulated.
512 devices in a mesh: bank: 16 (over x, z_hi), blk: 32 (over z_lo, y, core).
Axes of the slice: x: 4, y: 8, z: 8 (z_hi: 4, z_lo: 2; z = z_hi * 2 + z_lo), core: 2. Of those that a mesh axis runs over, the one named last changes fastest.
Arguments:
- k_store: bfloat16 [512, 512, 1024], P(('bank', 'blk')), may hold values from -6 to 6
- v_store: bfloat16 [512, 512, 1024], P(('bank', 'blk')), may hold values from -6 to 6
- pos_offset: int32 [512], replicated, may hold values from 0 to 8191
- owner_map: int32 [512], replicated, may hold values from 0 to 511, as said below
- passage_ids: int32 [32], replicated, may hold values from 0 to 511, as said below
- rec_index: int32 [32, 128], P('blk'), may hold values from 0 to 511, as said below
- rec_count: int32 [32], P('blk'), may hold values from 42 to 128, as said below
- fresh_q: bfloat16 [4096, 12288], P('blk', 'bank'), may hold values from -6 to 6
- fresh_k: bfloat16 [4096, 1024], P('blk'), may hold values from -6 to 6
- fresh_v: bfloat16 [4096, 1024], P('blk'), may hold values from -6 to 6
- ques_q: bfloat16 [512, 12288], P('blk', 'bank'), may hold values from -8 to 8
- ques_k: bfloat16 [512, 1024], P('blk'), may hold values from -8 to 8
- ques_v: bfloat16 [512, 1024], P('blk'), may hold values from -6 to 6
Outputs:
- rec_out: bfloat16 [4096, 12288], P('blk', 'bank')
- ques_out: bfloat16 [512, 12288], P('blk', 'bank')
Inputs may be any that keep to these rules, and one draw needn't show every extreme that they name: `owner_map`: a permutation of the 512 store slots; slot n lies on the device of flat index n over bank+blk. The slot owner_map[passage_ids[s]] equals o * 32 + s for some bank index o. `rec_index`: each row holds 128 distinct positions in rising order. `rec_count`: some passage uses all 128 slots in every draw.
All inputs are finite; a program needn't handle non-finite values.
Results may differ from a plain program's by a relative error of at most 0.017.
Values may be sent and summed in bfloat16 or wider, within the bound.
A program may use at most 64 MiB of HBM per device.

v0:
```python
import jax
import jax.numpy as jnp
from jax import lax
from jax.sharding import PartitionSpec as P

QH = 96
KVH = 8
HD = 128


rope_theta = 1000000.0
mask_floor = -1e30


def broadcast(array, axis, root):
    mine = lax.axis_index(axis) == root
    return lax.psum(jnp.where(mine, array, jnp.zeros_like(array)), axis)


def rotate(values, positions, head_dim):
    count = values.shape[0]
    heads = values.shape[1] // head_dim
    half = head_dim // 2
    parts = values.astype(jnp.float32).reshape(count, heads, head_dim)
    inverse = rope_theta ** (-jnp.arange(half).astype(jnp.float32) * 2.0 / head_dim)
    angles = positions.astype(jnp.float32)[:, None] * inverse[None, :]
    cosine = jnp.cos(angles)[:, None, :]
    sine = jnp.sin(angles)[:, None, :]
    first = parts[:, :, :half]
    second = parts[:, :, half:]
    turned = jnp.concatenate(
        [first * cosine - second * sine, second * cosine + first * sine], axis=2
    )
    return turned.reshape(count, heads * head_dim).astype(jnp.bfloat16)


def pick_block(total, limit):
    size = min(total, limit)
    while total % size != 0:
        size = size - 1
    return size


def attend(carry, queries, query_pos, keys, values, key_pos, head_dim):
    top, total, acc = carry
    count = keys.shape[0]
    kv_heads = queries.shape[1]
    key_view = keys.reshape(count, kv_heads, head_dim)
    value_view = values.reshape(count, kv_heads, head_dim)
    scores = jnp.einsum("rkgd,nkd->rkgn", queries, key_view, preferred_element_type=jnp.float32)
    scores = scores * (1.0 / float(head_dim) ** 0.5)
    allowed = key_pos[None, None, None, :] <= query_pos[:, None, None, None]
    scores = jnp.where(allowed, scores, mask_floor)
    new_top = jnp.maximum(top, jnp.max(scores, axis=-1))
    probs = jnp.where(allowed, jnp.exp(scores - new_top[..., None]), 0.0)
    factor = jnp.exp(top - new_top)
    total = total * factor + jnp.sum(probs, axis=-1)
    update = jnp.einsum(
        "rkgn,nkd->rkgd", probs.astype(jnp.bfloat16), value_view, preferred_element_type=jnp.float32
    )
    acc = acc * factor[..., None] + update
    return (new_top, total, acc)


def attend_blocks(carry, queries, query_pos, keys, values, key_pos, head_dim):
    count = keys.shape[0]
    size = pick_block(count, 1024)
    steps = count // size
    if steps == 1:
        return attend(carry, queries, query_pos, keys, values, key_pos, head_dim)

    def one_step(state, items):
        block_k, block_v, block_pos = items
        return (attend(state, queries, query_pos, block_k, block_v, block_pos, head_dim), None)

    width = keys.shape[1]
    carry, unused = lax.scan(
        one_step,
        carry,
        (
            keys.reshape(steps, size, width),
            values.reshape(steps, size, width),
            key_pos.reshape(steps, size),
        ),
    )
    return carry


def on_device(
    k_store,
    v_store,
    pos_offset,
    owner_map,
    passage_ids,
    rec_index,
    rec_count,
    fresh_q,
    fresh_k,
    fresh_v,
    ques_q,
    ques_k,
    ques_v,
):
    head_dim = HD
    group = QH // KVH
    cycle_size = lax.axis_size("blk")
    column = lax.axis_index("blk")
    bank_rank = lax.axis_index("bank")
    per_dev = k_store.shape[0]
    plen = k_store.shape[1]
    qlen_dev = ques_q.shape[0]
    rec_slots = rec_index.shape[1]
    local_heads = fresh_q.shape[1] // head_dim
    kv_local = max(1, local_heads // group)
    per_kv = local_heads // kv_local
    kv_first = bank_rank * local_heads // group
    kv_cols = kv_local * head_dim
    slot = owner_map[passage_ids[column]]
    owner = slot // (cycle_size * per_dev)
    within = slot % per_dev
    tokens = jnp.arange(plen).astype(jnp.int32)
    cached_pos = column * plen - pos_offset[slot] + tokens
    stored_k = lax.dynamic_index_in_dim(k_store, within, 0, keepdims=False)
    stored_v = lax.dynamic_index_in_dim(v_store, within, 0, keepdims=False)
    arrived_k, arrived_v = (broadcast(stored_k, "bank", owner), broadcast(stored_v, "bank", owner))
    own_k = lax.dynamic_slice_in_dim(arrived_k, kv_first * head_dim, kv_cols, 1)
    own_v = lax.dynamic_slice_in_dim(arrived_v, kv_first * head_dim, kv_cols, 1)
    own_k = rotate(own_k, cached_pos, head_dim)
    rec_local = rec_index[0]
    slot_rows = jnp.arange(rec_slots).astype(jnp.int32)
    valid = slot_rows < rec_count[0]
    target = jnp.where(valid, rec_local, plen)
    rec_pos = column * plen + rec_local
    new_keys = rotate(
        lax.dynamic_slice_in_dim(fresh_k, kv_first * head_dim, kv_cols, 1), rec_pos, head_dim
    )
    new_values = lax.dynamic_slice_in_dim(fresh_v, kv_first * head_dim, kv_cols, 1)
    pass_k = own_k.at[target].set(new_keys, mode="drop")
    pass_v = own_v.at[target].set(new_values, mode="drop")
    ques_pos = cycle_size * plen + column * qlen_dev + jnp.arange(qlen_dev).astype(jnp.int32)
    ques_keys = rotate(
        lax.dynamic_slice_in_dim(ques_k, kv_first * head_dim, kv_cols, 1), ques_pos, head_dim
    )
    ques_values = lax.dynamic_slice_in_dim(ques_v, kv_first * head_dim, kv_cols, 1)
    queries = jnp.concatenate(
        [rotate(fresh_q, rec_pos, head_dim), rotate(ques_q, ques_pos, head_dim)], axis=0
    )
    query_pos = jnp.concatenate([rec_pos, ques_pos], axis=0)
    rows = queries.shape[0]
    queries = queries.reshape(rows, kv_local, per_kv, head_dim)
    start_state = (
        jnp.full((rows, kv_local, per_kv), mask_floor, jnp.float32),
        jnp.zeros((rows, kv_local, per_kv), jnp.float32),
        jnp.zeros((rows, kv_local, per_kv, head_dim), jnp.float32),
    )
    span = plen + qlen_dev
    joined_k = jnp.concatenate([pass_k, ques_keys], axis=0)
    joined_v = jnp.concatenate([pass_v, ques_values], axis=0)
    pieces = (
        lax.all_gather(joined_k, "blk", axis=0, tiled=True),
        lax.all_gather(joined_v, "blk", axis=0, tiled=True),
    )
    index = jnp.arange(pieces[0].shape[0]).astype(jnp.int32)
    owner_dev = index // span
    offset = index % span
    key_pos = jnp.where(
        offset < plen,
        owner_dev * plen + offset,
        cycle_size * plen + owner_dev * qlen_dev + offset - plen,
    )
    final = attend_blocks(start_state, queries, query_pos, pieces[0], pieces[1], key_pos, head_dim)
    top, total, acc = final
    out = (acc / total[..., None]).reshape(rows, local_heads * head_dim)
    rec_out = jnp.where(valid[:, None], out[:rec_slots], 0.0).astype(jnp.bfloat16)
    ques_out = out[rec_slots:].astype(jnp.bfloat16)
    return (rec_out, ques_out)


def solution(mesh):
    return jax.shard_map(
        on_device,
        mesh=mesh,
        in_specs=(
            P(("bank", "blk"), None, None),
            P(("bank", "blk"), None, None),
            P(),
            P(),
            P(),
            P("blk", None),
            P("blk"),
            P("blk", "bank"),
            P("blk", None),
            P("blk", None),
            P("blk", "bank"),
            P("blk", None),
            P("blk", None),
        ),
        out_specs=(P("blk", "bank"), P("blk", "bank")),
        check_vma=False,
    )
```

profile of v0, /device:TPU:56, one launch (start us, length us, event | category | flops | bytes accessed | tf_op | source)
XLA Modules:
  0.0 486.2 jit_solution(13906572012612204573)
XLA Ops:
  7.2 1.3 dynamic_slice.41
  10.5 1.3 dynamic_slice.42
  14.4 1.5 copy.52
  16.5 1.4 select_bitcast_fusion
  20.2 1.3 dynamic_slice.44
  24.2 185.1 %all-reduce.3.cloned.1.call-done = (bf16[512,1024]{0,1:T(8,128)(2,1)}, bf16[512,1024]{0,1:T(8,128)(2,1)}) async-done(((bf16[512,1024]{0,1:T(8,128)(2,1)}, bf16[512,1024]{0,1:T(8,128)(2,1)}), (bf16[512,1024]{0,1:T(8,128)(2,1)}, bf16[512,1024]{0,1:T(8,128)(2,1)})) %all-reduce.3.cloned.1.call-update) | async-done | bytes 2097168 | tf_op jit(solution)/shard_map/psum | solution.py:17
  209.3 0.9 bitcast_convert_fusion
  210.9 1.0 scatter_fusion
  213.3 0.9 constant_dynamic-slice_fusion.1
  214.4 1.0 scatter_custom_fusion.1
  217.4 61.6 %all-gather.3.cloned.1.call-done = bf16[16896,128]{1,0:T(8,128)(2,1)} async-done(((bf16[528,128]{1,0:T(8,128)(2,1)}), bf16[16896,128]{1,0:T(8,128)(2,1)}) %all-gather.3.cloned.1.call-update) | async-done | bytes 4325392 | tf_op jit(solution)/shard_map/all_gather | solution.py:160
  279.1 71.6 %all-gather.5.cloned.1.call-done = bf16[16896,128]{1,0:T(8,128)(2,1)} async-done(((bf16[528,128]{1,0:T(8,128)(2,1)}), bf16[16896,128]{1,0:T(8,128)(2,1)}) %all-gather.5.cloned.1.call-update) | async-done | bytes 4325392 | tf_op jit(solution)/shard_map/all_gather | solution.py:161
  350.6 125.9 %while.15 = (s32[]{:T(128)}, f32[144,1,6]{0,2,1:T(8,128)S(1)}, f32[144,1,6]{0,2,1:T(8,128)S(1)}, f32[144,1,6,128]{3,0,2,1:T(8,128)}, s32[22,768]{1,0:T(8,128)S(1...) while((s32[]{:T(128)}, f32[144,1,6]{0,2,1:T(8,128)S(1)}, ...), condition=%wide.region_7.8_spmd.clone, body=%wide.region_4.7_spmd.clone.sunk | while | flops 348812352 | bytes 9970365 | solution.py:77
  350.8 1.7 fusion.73
  352.5 2.7 fusion.76
  355.2 0.9 fusion.75
  356.3 1.7 fusion.73
  358.0 2.9 fusion.76
  360.9 0.9 fusion.75
  362.1 1.7 fusion.73
  363.7 2.9 fusion.76
  366.7 0.9 fusion.75
  367.8 1.7 fusion.73
  369.5 2.9 fusion.76
  372.4 0.9 fusion.75
  373.5 1.7 fusion.73
  375.2 2.9 fusion.76
  379.3 1.7 fusion.73
  380.9 2.9 fusion.76
  385.0 1.7 fusion.73
  386.7 2.9 fusion.76
  390.7 1.7 fusion.73
  392.4 2.9 fusion.76
  396.5 1.7 fusion.73
  398.2 2.9 fusion.76
  402.2 1.7 fusion.73
  403.9 2.9 fusion.76
  407.9 1.7 fusion.73
  409.6 2.9 fusion.76
  413.7 1.7 fusion.73
  415.4 2.9 fusion.76
  419.4 1.7 fusion.73
  421.1 2.9 fusion.76
  424.0 0.9 fusion.75
  425.1 1.7 fusion.73
  426.8 2.9 fusion.76
  430.9 1.7 fusion.73
  432.6 2.9 fusion.76
  436.6 1.7 fusion.73
  438.3 2.9 fusion.76
  442.3 1.7 fusion.73
  444.0 2.9 fusion.76
  448.1 1.7 fusion.73
  449.8 2.9 fusion.76
  453.8 1.7 fusion.73
  455.5 2.9 fusion.76
  458.4 0.9 fusion.75
  459.5 1.7 fusion.73
  461.2 2.9 fusion.76
  465.3 1.7 fusion.73
  467.0 2.9 fusion.76
  471.0 1.7 fusion.73
  472.7 2.9 fusion.76
  476.6 1.3 copy.62
  (186 shorter events, 27.1 us)
Async XLA Ops:
  7.2 207.2 %copy-start = (bf16[128,1024]{1,0:T(8,128)(2,1)S(1)}, bf16[128,1024]{1,0:T(8,128)(2,1)}, u32[]{:S(2)}) copy-start(bf16[128,1024]{1,0:T(8,128)(2,1)} %param.24) | copy-start | bytes 786436
  7.2 8.7 %copy-start.1 = (bf16[1,512,1024]{2,1,0:T(8,128)(2,1)S(1)}, bf16[1,512,1024]{2,1,0:T(8,128)(2,1)}, u32[]{:S(2)}) copy-start(bf16[1,512,1024]{2,1,0:T(8,128)(2,1)} %param.16) | copy-start | bytes 3145732
  7.2 202.1 %all-reduce.3.cloned.1.call-start = ((), (), s32[]{:S(2)}) async-start(), calls=%async_computation.2 | async-start | bytes 4194304 | tf_op jit(solution)/shard_map/psum | solution.py:17
  16.5 5.7 %copy-start.4 = (s32[1,128]{1,0:T(1,128)S(1)}, s32[1,128]{1,0:T(1,128)}, u32[]{:S(2)}) copy-start(s32[1,128]{1,0:T(1,128)} %param.20) | copy-start | bytes 1540
  17.9 198.2 %copy-start.2 = (bf16[128,768]{1,0:T(8,128)(2,1)S(1)}, bf16[128,768]{1,0:T(8,128)(2,1)}, u32[]{:S(2)}) copy-start(bf16[128,768]{1,0:T(8,128)(2,1)} %param.22) | copy-start | bytes 589828
  18.0 198.4 %copy-start.3 = (bf16[16,768]{1,0:T(8,128)(2,1)S(1)}, bf16[16,768]{1,0:T(8,128)(2,1)}, u32[]{:S(2)}) copy-start(bf16[16,768]{1,0:T(8,128)(2,1)} %param.25) | copy-start | bytes 73732
  18.0 261.1 %all-gather.3.cloned.1.call-start = ((), (), s32[]{:S(2)}) async-start(), calls=%async_computation | async-start | bytes 4460544 | tf_op jit(solution)/shard_map/all_gather | solution.py:160
  212.6 138.0 %all-gather.5.cloned.1.call-start = ((), (), s32[]{:S(2)}) async-start(), calls=%async_computation.1 | async-start | bytes 4460544 | tf_op jit(solution)/shard_map/all_gather | solution.py:161
Sparse Core Ops, SparseCore 0:
  18.1 191.1 all-reduce.2
  212.7 66.2 all-gather.2
  281.2 69.3 all-gather.4
where the time goes:
time: 491 us; the launch traced here: 486 us
  waiting for transfers between devices  318 us (65%)
  matrix products  101 us (21%)
  other arithmetic  29.6 us (6%)
  between operations  21.3 us (4%)
  local copies, waits for them, and re-layouts  14.7 us (3%)
    psum x1, waiting for transfers between devices, broadcast(): return lax.psum(jnp.where(mine, array, jnp.zeros_like(array)), axis)  185 us
    all_gather x1, waiting for transfers between devices, on_device(): lax.all_gather(joined_v, 'blk', axis=0, tiled=True)  71.6 us
    dot_general x22, matrix products, attend(): jnp.einsum('rkgn,nkd->rkgd', probs.astype(jnp.bfloat16), value_view, pref...  64.3 us
    all_gather x1, waiting for transfers between devices, on_device(): lax.all_gather(joined_k, 'blk', axis=0, tiled=True)  61.6 us
    dot_general x22, matrix products, attend(): jnp.einsum('rkgd,nkd->rkgn', queries, key_view, preferred_element_type=jn...  36.7 us
    reduce_sum x22, other arithmetic, attend(): total = total * factor + jnp.sum(probs, axis=-1)  20 us
  transfers between devices with their start and end apart: 3, of which 3 were waited for; matrix products, arithmetic and copies ran while one was open for 2% of the time, Pallas kernels for 0%

commit v1 on v0

v1 whole, which is shorter than its diff:
```python
import functools

import jax
import jax.numpy as jnp
import numpy as np
from jax import lax
from jax.experimental import pallas as pl
from jax.experimental.pallas import tpu as pltpu
from jax.sharding import PartitionSpec as P

HD = 128
PT = 512
RECP = 128
QDEV = 16
PASS = 32
HEADS = 6
ROWS = HEADS * RECP
QROWS = HEADS * QDEV
QSTART = PASS * PT
CHUNK = 512
FLOOR = -1e30
SCALE = float(np.log2(np.e) / np.sqrt(128.0))
MESH = pl.DeviceIdType.MESH
F32 = jnp.float32
BF16 = jnp.bfloat16

INV_2PI = float(1.0 / (2.0 * np.pi))
PI_A = 6.28125
PI_B = 0.0019350051879882812
PI_C = 3.0199159795074593e-07
SIN_C = [float((-1.0) ** k / np.prod(np.arange(1, 2 * k + 2, dtype=np.float64))) for k in range(9)]
COS_C = [float((-1.0) ** k / np.prod(np.arange(1, 2 * k + 1, dtype=np.float64))) for k in range(10)]


def freq_table():
    half = HD // 2
    freqs = 1000000.0 ** (-np.arange(half, dtype=np.float64) * 2.0 / HD)
    return np.concatenate([freqs, freqs])[None, :].astype(np.float32)


def cos_sin(pos, freq):
    angle = pos * freq
    turns = jnp.floor(angle * INV_2PI + 0.5)
    r = ((angle - turns * PI_A) - turns * PI_B) - turns * PI_C
    r2 = r * r
    s = jnp.full_like(r, SIN_C[8])
    for k in range(7, -1, -1):
        s = s * r2 + SIN_C[k]
    s = s * r
    c = jnp.full_like(r, COS_C[9])
    for k in range(8, -1, -1):
        c = c * r2 + COS_C[k]
    lane = lax.broadcasted_iota(jnp.int32, s.shape, 1)
    return c, jnp.where(lane < HD // 2, -s, s)


def turn(x, c, s):
    return x * c + pltpu.roll(x, HD // 2, 1) * s


def eye_mask(n, m):
    row = lax.broadcasted_iota(jnp.int32, (n, m), 0)
    col = lax.broadcasted_iota(jnp.int32, (n, m), 1)
    return row == col


def to_col(row, n):
    full = jnp.broadcast_to(row, (n, 128))
    return jnp.sum(jnp.where(eye_mask(n, 128), full, 0.0), axis=1, keepdims=True)


def to_row(col, n):
    return jnp.sum(jnp.where(eye_mask(n, 128), col, 0.0), axis=0, keepdims=True)


def nt_dot(a, b):
    return lax.dot_general(a, b, (((1,), (1,)), ((), ())), preferred_element_type=F32)


def kernel(
    pos_off, owner_map, pids, rec_count, rec_index, fresh_q, fresh_k, fresh_v,
    ques_q, ques_k, ques_v, freq_ref, k_store, v_store,
    rec_out, ques_out,
    xfin0, xfin1, mb00, mb01, mb10, mb11, msend, zsend, zin0, zin1, tab, hit, kall, vall, kq, vq,
    qrec, qques, qpos, sbuf, sq, osend, oqsend, orecv, oqrecv, lsend, lrecv,
    lsem, xs, xr, zs, zr, qs, qr, ps, pr, ns, nr, cs, cr, os_, or_,
):
    bank = lax.axis_index("bank")
    blk = lax.axis_index("blk")
    x = lax.div(bank, 4)
    z_hi = lax.rem(bank, 4)
    zh = lax.div(z_hi, 2)
    b1 = lax.rem(z_hi, 2)
    z_lo = lax.div(blk, 16)
    g = lax.rem(blk, 16)
    y = lax.div(g, 2)
    core = lax.rem(g, 2)
    zc = 2 * z_hi + z_lo
    z4 = 2 * b1 + z_lo
    head = 2 * x + zh

    def dev(xx, zz, gg):
        return (xx * 4 + lax.div(zz, 2), lax.rem(zz, 2) * 16 + gg)

    x_up = dev(lax.rem(x + 1, 4), zc, g)
    x_dn = dev(lax.rem(x + 3, 4), zc, g)
    y_up = dev(x, zc, lax.rem(y + 1, 8) * 2 + core)
    y_dn = dev(x, zc, lax.rem(y + 7, 8) * 2 + core)
    twin = dev(x, zc, y * 2 + 1 - core)

    def z_dev(i):
        return dev(x, lax.rem(zc + i, 8), g)

    def z4_dev(i):
        return dev(x, 4 * zh + lax.rem(z4 + i, 4), g)

    def rcopy(src, dst, ssem, rsem, where):
        return pltpu.make_async_remote_copy(
            src_ref=src, dst_ref=dst, send_sem=ssem, recv_sem=rsem,
            device_id=where, device_id_type=MESH,
        )

    xfin = (xfin0, xfin1)
    mbuf = ((mb00, mb01), (mb10, mb11))
    zin = (zin0, zin1)

    def slot_of(passage):
        return owner_map[pids[passage]]

    slot = slot_of(blk)
    owner_x = lax.div(slot, 128)
    off = pos_off[slot]
    count = rec_count[0]

    barrier = pltpu.get_barrier_semaphore()
    peers = [x_up, x_dn, y_up, y_dn, twin] + [z_dev(i) for i in range(1, 8)]
    for peer in peers:
        pl.semaphore_signal(barrier, inc=1, device_id=peer, device_id_type=MESH)
    pl.semaphore_wait(barrier, len(peers))

    stores = (k_store, v_store)

    def cols(xx):
        return pl.ds(pl.multiple_of(lax.rem(xx, 4) * 256, 256), 256)

    top = pl.ds(0, 256)
    low = pl.ds(256, 256)

    def x_first(part):
        st = stores[part].at[0]
        copies = [
            rcopy(st.at[top, cols(x + 2)], mbuf[part][0].at[1], xs.at[part, 0], xr.at[part, 0], x_up),
            rcopy(st.at[low, cols(x + 2)], mbuf[part][1].at[1], xs.at[part, 1], xr.at[part, 1], x_dn),
            rcopy(st.at[low, cols(x + 1)], xfin[part].at[1, 1], xs.at[part, 2], xr.at[part, 2], x_up),
            rcopy(st.at[top, cols(x + 3)], xfin[part].at[2, 0], xs.at[part, 3], xr.at[part, 3], x_dn),
        ]
        for c in copies:
            c.start()
        return copies

    def x_local(part):
        st = stores[part].at[0]
        copies = [
            pltpu.make_async_copy(st.at[top, cols(x + 1)], mbuf[part][0].at[0], lsem.at[part, 0]),
            pltpu.make_async_copy(st.at[low, cols(x + 3)], mbuf[part][1].at[0], lsem.at[part, 1]),
            pltpu.make_async_copy(st.at[top, cols(x)], xfin[part].at[0, 0], lsem.at[part, 2]),
            pltpu.make_async_copy(st.at[low, cols(x)], xfin[part].at[0, 1], lsem.at[part, 3]),
        ]
        for c in copies:
            c.start()
        return copies

    def x_second(part, first, local):
        local[0].wait()
        first[0].wait_recv()
        from_dn = jnp.where(owner_x == lax.rem(x + 3, 4), 1, 0)
        msend[part, 0] = mbuf[part][0][from_dn]
        c4 = rcopy(msend.at[part, 0], xfin[part].at[1, 0], xs.at[part, 4], xr.at[part, 4], x_up)
        c4.start()
        local[1].wait()
        first[1].wait_recv()
        from_up = jnp.where(owner_x == lax.rem(x + 1, 4), 1, 0)
        msend[part, 1] = mbuf[part][1][from_up]
        c5 = rcopy(msend.at[part, 1], xfin[part].at[2, 1], xs.at[part, 5], xr.at[part, 5], x_dn)
        c5.start()
        return [c4, c5]

    def x_finish(part, first, second, local):
        local[2].wait()
        local[3].wait()
        first[2].wait_recv()
        first[3].wait_recv()
        for c in second:
            c.wait_recv()
        is_own = owner_x == x
        idx_a = jnp.where(is_own, 0, jnp.where(owner_x == lax.rem(x + 1, 4), 2, 1))
        idx_b = jnp.where(is_own, 0, jnp.where(owner_x == lax.rem(x + 3, 4), 1, 2))
        fresh = (fresh_k, fresh_v)[part]
        fcols = fresh[:, cols(x)]
        for quarter in range(4):
            half, r0 = quarter // 2, (quarter % 2) * 128
            idx = idx_a if half == 0 else idx_b
            data = xfin[part][idx, half, r0:r0 + 128, :].astype(F32)
            onehot = hit[quarter]
            repl = jnp.dot(onehot, fcols, preferred_element_type=F32)
            found = jnp.sum(onehot.astype(F32), axis=1, keepdims=True) > 0.5
            data = jnp.where(found, repl, data)
            for hh in range(2):
                piece = data[:, hh * 128:(hh + 1) * 128]
                if part == 0:
                    piece = turn(piece, tab[quarter, 0], tab[quarter, 1])
                zsend[part, quarter, hh] = piece.astype(BF16)
        copies = []
        for i in range(1, 8):
            t = lax.rem(zc + i, 8)
            c = rcopy(
                zsend.at[part, lax.rem(t, 4), lax.div(t, 4)], zin[part].at[i],
                zs.at[part, i - 1], zr.at[part, i - 1], z_dev(i),
            )
            c.start()
            copies.append(c)
        zin[part][0] = zsend[part, z4, zh]
        return copies

    def z_finish(part, copies):
        for c in copies:
            c.wait_recv()
        for c in range(2):
            owner_z = lax.rem(lax.div(slot_of(c * 16 + g), 32), 4)
            idx = lax.rem(zc + 8 - (2 * owner_z + c), 8)
            block = zin[part][idx]
            rows = pl.ds(pl.multiple_of(g * 128, 128), 128)
            if part == 0:
                kall[c, rows, :] = block
            else:
                vall[c, rows, 0:128] = block

    def gather_slices(fam, gg):
        if fam == 0:
            return kall.at[:, pl.ds(pl.multiple_of(gg * 128, 128), 128), :]
        if fam == 1:
            return vall.at[:, pl.ds(pl.multiple_of(gg * 128, 128), 128), pl.ds(0, 128)]
        if fam == 2:
            return kq.at[pl.ds(pl.multiple_of(gg * 16, 16), 16), :]
        return vq.at[pl.ds(pl.multiple_of(gg * 16, 16), 16), pl.ds(0, 128)]

    def reach(fam):
        return (4, 3) if fam % 2 == 0 else (3, 4)

    def at_y(dy):
        return lax.rem(y + 8 + dy, 8) * 2 + core

    sent = []

    def g_send(fam, dy, which, hop):
        piece = gather_slices(fam, at_y(dy))
        if which == "up":
            c = rcopy(piece, piece, ps.at[fam, hop], pr.at[fam, hop], y_up)
        elif which == "dn":
            c = rcopy(piece, piece, ns.at[fam, hop], nr.at[fam, hop], y_dn)
        else:
            c = rcopy(piece, piece, cs.at[fam, hop], cr.at[fam, hop], twin)
        c.start()
        sent.append(c)

    def g_wait(fam, dy, which, hop):
        if which == "up":
            piece = gather_slices(fam, at_y(dy))
            rcopy(piece, piece, ps.at[fam, hop], pr.at[fam, hop], y_up).wait_recv()
        elif which == "dn":
            piece = gather_slices(fam, at_y(dy))
            rcopy(piece, piece, ns.at[fam, hop], nr.at[fam, hop], y_dn).wait_recv()
        else:
            piece = gather_slices(fam, lax.rem(y + 8 + dy, 8) * 2 + 1 - core)
            rcopy(piece, piece, cs.at[fam, hop], cr.at[fam, hop], twin).wait_recv()

    def g_start(fam):
        g_send(fam, 0, "up", 0)
        g_send(fam, 0, "dn", 0)
        g_send(fam, 0, "twin", 0)

    def g_step(fam, d):
        n_up, n_dn = reach(fam)
        if d <= n_up:
            g_wait(fam, -d, "up", d - 1)
            if d < n_up:
                g_send(fam, -d, "up", d)
            g_send(fam, -d, "twin", d)
        if d <= n_dn:
            g_wait(fam, d, "dn", d - 1)
            if d < n_dn:
                g_send(fam, d, "dn", d)
            g_send(fam, d, "twin", d if d == 4 else 4 + d)

    def g_end(fam):
        n_up, n_dn = reach(fam)
        g_wait(fam, 0, "twin", 0)
        for d in range(1, n_up + 1):
            g_wait(fam, -d, "twin", d)
        for d in range(1, n_dn + 1):
            g_wait(fam, d, "twin", d if d == 4 else 4 + d)

    loc_k = x_local(0)
    first_k = x_first(0)
    loc_v = x_local(1)

    freq = freq_ref[...]
    rec_row = rec_index[...].astype(F32)
    rec_pos_row = rec_row + (blk * PT).astype(F32)
    rec_pos = to_col(rec_pos_row, 128)
    c_rec, s_rec = cos_sin(rec_pos, freq)
    ques_pos = (
        lax.broadcasted_iota(jnp.int32, (QDEV, 1), 0) + (QSTART + blk * QDEV)
    ).astype(F32)
    c_q, s_q = cos_sin(ques_pos, freq)
    for hh in range(HEADS):
        lanes = slice(hh * 128, (hh + 1) * 128)
        q = turn(fresh_q[:, lanes].astype(F32), c_rec, s_rec) * SCALE
        qrec[z4, hh * 128:(hh + 1) * 128, :] = q.astype(BF16)
        q = turn(ques_q[:, lanes].astype(F32), c_q, s_q) * SCALE
        qques[z4, hh * 16:(hh + 1) * 16, :] = q.astype(BF16)
    qpos[z4] = jnp.broadcast_to(rec_pos_row, (8, 128))
    q_copies = []
    for i in range(1, 4):
        for j, ref in enumerate((qrec, qques, qpos)):
            c = rcopy(ref.at[z4], ref.at[z4], qs.at[i - 1, j], qr.at[i - 1, j], z4_dev(i))
            c.start()
            q_copies.append((i, j, c))

    vall[:, :, 128:256] = jnp.ones((2, 2048, 128), BF16)
    vq[:, 128:256] = jnp.ones((256, 128), BF16)
    hcol = pl.ds(pl.multiple_of(head * 128, 128), 128)
    my_rows = pl.ds(pl.multiple_of(g * 16, 16), 16)
    kq[my_rows, :] = turn(ques_k[:, hcol].astype(F32), c_q, s_q).astype(BF16)
    vq[my_rows, 0:128] = ques_v[:, hcol]

    second_k = x_second(0, first_k, loc_k)
    first_v = x_first(1)
    g_start(2)
    g_start(3)

    off_f = off.astype(F32)
    base_f = (blk * PT).astype(F32)
    slot_lane = lax.broadcasted_iota(jnp.int32, (128, 128), 1)
    for quarter in range(4):
        tok = lax.broadcasted_iota(jnp.int32, (128, 128), 0) + quarter * 128
        match = (tok.astype(F32) == jnp.broadcast_to(rec_row, (128, 128))) & (slot_lane < count)
        onehot = jnp.where(match, 1.0, 0.0)
        hit[quarter] = onehot.astype(BF16)
        found = jnp.sum(onehot, axis=1, keepdims=True) > 0.5
        tpos = (lax.broadcasted_iota(jnp.int32, (128, 1), 0) + quarter * 128).astype(F32) + base_f
        tpos = tpos - jnp.where(found, 0.0, off_f)
        c_t, s_t = cos_sin(tpos, freq)
        tab[quarter, 0] = c_t
        tab[quarter, 1] = s_t

    z_k = x_finish(0, first_k, second_k, loc_k)
    second_v = x_second(1, first_v, loc_v)
    for d in range(1, 5):
        g_step(2, d)
        g_step(3, d)
    z_finish(0, z_k)
    g_start(0)
    z_v = x_finish(1, first_v, second_v, loc_v)
    for d in range(1, 5):
        g_step(0, d)
    z_finish(1, z_v)
    g_start(1)
    for d in range(1, 5):
        g_step(1, d)
    for fam in range(4):
        g_end(fam)
    for i, j, c in q_copies:
        c.wait_recv()

    lsend[...] = jnp.zeros((4, 8, 128), F32)
    key_lane = lax.broadcasted_iota(jnp.int32, (1, CHUNK), 1)
    key_off = lax.div(key_lane, 128) * PT + lax.rem(key_lane, 128) + z4 * 128
    key_off = key_off.astype(F32)

    def k_chunk(ch):
        return kall[lax.div(ch, 4), pl.ds(pl.multiple_of(lax.rem(ch, 4) * CHUNK, CHUNK), CHUNK), :]

    def v_chunk(ch):
        return vall[lax.div(ch, 4), pl.ds(pl.multiple_of(lax.rem(ch, 4) * CHUNK, CHUNK), CHUNK), :]

    def fold(s):
        m = s[:, 0:128]
        for j in range(1, s.shape[1] // 128):
            m = jnp.maximum(m, s[:, j * 128:(j + 1) * 128])
        return m

    def scores(q, ch, rows, m):
        s = nt_dot(q, k_chunk(ch))
        sbuf[ch, 0:rows, :] = s
        return jnp.maximum(m, fold(s))

    def weigh(ch, rows, m, acc):
        p = jnp.exp2(sbuf[ch, 0:rows, :] - m).astype(BF16)
        return acc + jnp.dot(p, v_chunk(ch), preferred_element_type=F32)

    qq = qques[...].reshape(4 * QROWS, 128)
    m = jnp.full((4 * QROWS, 128), FLOOR, F32)
    m = lax.fori_loop(0, 8, lambda ch, mm: scores(qq, ch, 4 * QROWS, mm), m)
    s = nt_dot(qq, kq[...])
    row = lax.broadcasted_iota(jnp.int32, (4 * QROWS, 1), 0)
    row_src = lax.div(row, QROWS)
    row_pos = lax.rem(row_src, 2) * 256 + g * 16 + lax.rem(row, 16)
    col = lax.broadcasted_iota(jnp.int32, (1, 256), 1)
    col_pos = z_lo * 256 + col
    col_mine = lax.div(lax.rem(col, 16), 8) == b1
    col_pos = jnp.where(col_mine, col_pos, 100000)
    s = jnp.where(col_pos <= row_pos, s, FLOOR)
    sq[...] = s
    m = jnp.max(jnp.maximum(m, fold(s)), axis=1, keepdims=True)
    acc = jnp.zeros((4 * QROWS, 256), F32)
    acc = lax.fori_loop(0, 8, lambda ch, a: weigh(ch, 4 * QROWS, m, a), acc)
    p = jnp.exp2(sq[...] - m).astype(BF16)
    acc = acc + jnp.dot(p, vq[...], preferred_element_type=F32)
    total = acc[:, 128:256]
    o = (acc[:, 0:128] / total).astype(BF16)
    lse = m + jnp.log2(total)
    for src in range(4):
        rows = slice(src * QROWS, (src + 1) * QROWS)
        oqsend[src] = o[rows]
        lsend[src, 6:7, :] = to_row(lse[rows], QROWS)
    oqrecv[z4] = oqsend[z4]
    out_copies = []
    for i in range(1, 4):
        src = lax.rem(z4 + i, 4)
        c = rcopy(oqsend.at[src], oqrecv.at[z4], os_.at[i - 1, 1], or_.at[i - 1, 1], z4_dev(i))
        c.start()
        out_copies.append(c)

    def rec_tile(i):
        src = lax.rem(z4 + i, 4)
        c = lax.rem(src, 2)
        n_open = 4 * c + lax.div(g, 4)
        q = qrec[src]
        m = jnp.full((ROWS, 128), FLOOR, F32)
        m = lax.fori_loop(0, n_open, lambda ch, mm: scores(q, ch, ROWS, mm), m)
        pos_col = to_col(qpos[src, 0:1, :], 128)
        seen = (key_off + (n_open * (4 * PT)).astype(F32)) <= pos_col
        k_last = k_chunk(n_open)
        tops = []
        for hh in range(HEADS):
            s = nt_dot(q[hh * 128:(hh + 1) * 128], k_last)
            s = jnp.where(seen, s, FLOOR)
            sbuf[n_open, hh * 128:(hh + 1) * 128, :] = s
            tops.append(fold(s))
        m = jnp.max(jnp.maximum(m, jnp.concatenate(tops, axis=0)), axis=1, keepdims=True)
        acc = jnp.zeros((ROWS, 256), F32)
        acc = lax.fori_loop(0, n_open + 1, lambda ch, a: weigh(ch, ROWS, m, a), acc)
        total = acc[:, 128:256]
        o = (acc[:, 0:128] / total).astype(BF16)
        lse = m + jnp.log2(total)
        for hh in range(HEADS):
            lsend[src, hh:hh + 1, :] = to_row(lse[hh * 128:(hh + 1) * 128], 128)
        return src, o

    for i in range(1, 4):
        src, o = rec_tile(i)
        osend[i - 1] = o
        c = rcopy(osend.at[i - 1], orecv.at[z4], os_.at[i - 1, 0], or_.at[i - 1, 0], z4_dev(i))
        c.start()
        out_copies.append(c)
        c = rcopy(lsend.at[src], lrecv.at[z4], os_.at[i - 1, 2], or_.at[i - 1, 2], z4_dev(i))
        c.start()
        out_copies.append(c)
    src, o = rec_tile(0)
    orecv[z4] = o
    lrecv[z4] = lsend[z4]

    for c in out_copies:
        c.wait_recv()

    def join(parts, lses, n):
        cols_ = [to_col(l, n) for l in lses]
        top_ = functools.reduce(jnp.maximum, cols_)
        ws = [jnp.exp2(c - top_) for c in cols_]
        total = ws[0] + ws[1] + ws[2] + ws[3]
        acc = ws[0] * parts[0].astype(F32)
        for w, part in zip(ws[1:], parts[1:]):
            acc = acc + w * part.astype(F32)
        return acc / total

    used = lax.broadcasted_iota(jnp.int32, (128, 1), 0) < count
    for hh in range(HEADS):
        rows = slice(hh * 128, (hh + 1) * 128)
        o = join([orecv[j, rows, :] for j in range(4)], [lrecv[j, hh:hh + 1, :] for j in range(4)], 128)
        rec_out[:, rows] = jnp.where(used, o, 0.0).astype(BF16)
    o = join([oqrecv[j] for j in range(4)], [lrecv[j, 6:7, :] for j in range(4)], QROWS)
    for hh in range(HEADS):
        ques_out[:, hh * 128:(hh + 1) * 128] = o[hh * 16:(hh + 1) * 16].astype(BF16)

    for c in first_k + second_k + first_v + second_v + z_k + z_v:
        c.wait_send()
    for i, j, c in q_copies:
        c.wait_send()
    for c in sent + out_copies:
        c.wait_send()


def on_device(
    k_store, v_store, pos_offset, owner_map, passage_ids, rec_index, rec_count,
    fresh_q, fresh_k, fresh_v, ques_q, ques_k, ques_v,
):
    vmem = pl.BlockSpec(memory_space=pltpu.VMEM)
    smem = pl.BlockSpec(memory_space=pltpu.SMEM)
    anym = pl.BlockSpec(memory_space=pl.ANY)
    dma = pltpu.SemaphoreType.DMA
    v = pltpu.VMEM
    return pl.pallas_call(
        kernel,
        out_shape=(
            jax.ShapeDtypeStruct((RECP, HEADS * HD), BF16),
            jax.ShapeDtypeStruct((QDEV, HEADS * HD), BF16),
        ),
        in_specs=[smem] * 4 + [vmem] * 8 + [anym] * 2,
        out_specs=(vmem, vmem),
        scratch_shapes=[
            v((3, 2, 256, 256), BF16), v((3, 2, 256, 256), BF16),
            v((2, 256, 256), BF16), v((2, 256, 256), BF16),
            v((2, 256, 256), BF16), v((2, 256, 256), BF16),
            v((2, 2, 256, 256), BF16),
            v((2, 4, 2, 128, 128), BF16),
            v((8, 128, 128), BF16), v((8, 128, 128), BF16),
            v((4, 2, 128, 128), F32),
            v((4, 128, 128), BF16),
            v((2, 2048, 128), BF16),
            v((2, 2048, 256), BF16),
            v((256, 128), BF16),
            v((256, 256), BF16),
            v((4, ROWS, 128), BF16),
            v((4, QROWS, 128), BF16),
            v((4, 8, 128), F32),
            v((8, ROWS, CHUNK), F32),
            v((4 * QROWS, 256), F32),
            v((3, ROWS, 128), BF16),
            v((4, QROWS, 128), BF16),
            v((4, ROWS, 128), BF16),
            v((4, QROWS, 128), BF16),
            v((4, 8, 128), F32),
            v((4, 8, 128), F32),
            dma((2, 4)),
            dma((2, 6)), dma((2, 6)),
            dma((2, 7)), dma((2, 7)),
            dma((3, 3)), dma((3, 3)),
            dma((4, 4)), dma((4, 4)),
            dma((4, 4)), dma((4, 4)),
            dma((4, 8)), dma((4, 8)),
            dma((3, 3)), dma((3, 3)),
        ],
        compiler_params=pltpu.CompilerParams(
            collective_id=0, has_side_effects=True, vmem_limit_bytes=50 * 1024 * 1024
        ),
        cost_estimate=pl.CostEstimate(
            flops=8_000_000_000, bytes_accessed=4_000_000, transcendentals=15_000_000
        ),
        name="blend_attend",
    )(
        pos_offset, owner_map, passage_ids, rec_count, rec_index, fresh_q, fresh_k, fresh_v,
        ques_q, ques_k, ques_v, jnp.asarray(freq_table()), k_store, v_store,
    )


def solution(mesh):
    return jax.shard_map(
        on_device,
        mesh=mesh,
        in_specs=(
            P(("bank", "blk"), None, None),
            P(("bank", "blk"), None, None),
            P(),
            P(),
            P(),
            P("blk", None),
            P("blk"),
            P("blk", "bank"),
            P("blk", None),
            P("blk", None),
            P("blk", "bank"),
            P("blk", None),
            P("blk", None),
        ),
        out_specs=(P("blk", "bank"), P("blk", "bank")),
        check_vma=False,
    )
```

time: 491 us -> 114 us (0.23)
  waiting for transfers between devices: 318 us -> 0 us
  matrix products: 101 us -> 0 us
  Pallas kernels: 0 us -> 101 us
  other arithmetic: 29.6 us -> 0 us
  between operations: 21.3 us -> 1.38 us
    psum x1 -> x0, waiting for transfers between devices: 185 us -> none  [broadcast(): return lax.psum(jnp.where(mine, array, jnp.zeros_like(array)), axis)]
    all_gather x2 -> x0, waiting for transfers between devices: 133 us -> none  [the longest x1 71.6 us: on_device(): lax.all_gather(joined_v, 'blk', axis=0, tiled=True)]
    pallas_call x0 -> x1, Pallas kernels: none -> 101 us  [on_device(): pl.pallas_call(kernel, out_shape=(jax.ShapeDtypeStruct((RECP, HEADS * HD)...]
    dot_general x44 -> x0, matrix products: 101 us -> none  [the longest x22 64.3 us: attend(): jnp.einsum('rkgn,nkd->rkgd', probs.astype(jnp.bfloat16), value_view, pref...]
    reduce_sum x22 -> x0, other arithmetic: 20 us -> none  [attend(): total = total * factor + jnp.sum(probs, axis=-1)]
    dynamic_slice x29 -> x0, local copies, waits for them, and re-layouts: 6.82 us -> none  [the longest x2 2.6 us: on_device(): slot = owner_map[passage_ids[column]]]
    unnamed x16 -> x28, local copies, waits for them, and re-layouts: 3.38 us -> 10.2 us
  transfers between devices with their start and end apart: 3 -> 0, of which waited for: 3 -> 0; matrix products, arithmetic and copies ran while one was open for 2% -> 0% of each run, Pallas kernels for 0% -> 0%
where the time goes in v1:
time: 114 us; the launch traced here: 113 us
  Pallas kernels  101 us (89%)
  local copies, waits for them, and re-layouts  10.2 us (9%)
  between operations  1.38 us (1%)
    pallas_call x1, Pallas kernels, on_device(): pl.pallas_call(kernel, out_shape=(jax.ShapeDtypeStruct((RECP, HEADS * HD)...  101 us
    unnamed x28, local copies, waits for them, and re-layouts  10.2 us

profile of v1, /device:TPU:56, one launch (start us, length us, event | category | flops | bytes accessed | tf_op | source)
XLA Modules:
  0.0 112.7 jit_solution(15050822500096938080)
XLA Ops:
  0.6 0.0 copy-start.12
  0.6 0.0 copy-start.11
  0.7 0.0 copy-start.10
  1.3 0.0 copy-done.12
  1.3 0.0 copy-done.11
  1.4 0.0 copy-done.10
  1.4 0.0 copy-start
  1.4 1.2 %copy-done = bf16[1,512,1024]{2,1,0:T(8,128)(2,1)S(1)} copy-done((bf16[1,512,1024]{2,1,0:T(8,128)(2,1)S(1)}, bf16[1,512,1024]{2,1,0:T(8,128)(2,1)}, u32[]{:S(2)}) %copy-start) | copy-done | bytes 1048600
  2.6 0.0 copy-start.1
  2.6 1.2 %copy-done.1 = bf16[1,512,1024]{2,1,0:T(8,128)(2,1)S(1)} copy-done((bf16[1,512,1024]{2,1,0:T(8,128)(2,1)S(1)}, bf16[1,512,1024]{2,1,0:T(8,128)(2,1)}, u32[]{:S(2)}) %copy-start.1) | copy-done | bytes 1048600
  3.8 0.0 copy-start.2
  3.8 0.9 copy-done.2
  4.8 0.0 copy-start.3
  4.8 0.9 copy-done.3
  5.7 0.0 copy-start.4
  5.7 0.9 copy-done.4
  6.6 0.0 copy-start.5
  6.6 0.8 copy-done.5
  7.4 0.0 copy-start.6
  7.4 0.8 copy-done.6
  8.2 0.0 copy-start.7
  8.2 0.7 copy-done.7
  8.9 0.0 copy-start.8
  8.9 0.7 copy-done.8
  9.6 0.0 copy-start.9
  9.6 0.7 copy-done.9
  10.3 101.1 %blend_attend.1 = (bf16[128,768]{1,0:T(8,128)(2,1)S(1)}, bf16[16,768]{1,0:T(8,128)(2,1)S(1)}) custom-call(s32[512]{0:T(512)S(1)} %copy-done.8, s32[512]{0:T(512)S(1)} %copy-done.9, s32[32]{0:T(128)S(1)} %copy-done.10, s32[1]{0:T(128)S(6)} %copy.18.rec_count, s32[1,128]{1,0:T(1,128)S(1)} %copy-done.11, bf16[128,768]{1,0:T(8,128)(2,1)S(1)} %copy-done.4, ...), custom_call_target="tpu_custom_call" | custom-call | flops 8000000000 | bytes 4000000 | tf_op jit(solution)/shard_map/blend_attend/pallas_call | solution.py:513
  111.4 0.7 copy.19
  112.1 0.6 copy.20
Async XLA Ops:
  0.6 0.7 copy-start.12
  0.6 0.7 copy-start.11
  0.7 0.7 copy-start.10
  1.4 1.2 %copy-start = (bf16[1,512,1024]{2,1,0:T(8,128)(2,1)S(1)}, bf16[1,512,1024]{2,1,0:T(8,128)(2,1)}, u32[]{:S(2)}) copy-start(bf16[1,512,1024]{2,1,0:T(8,128)(2,1)} %k_store.1) | copy-start | bytes 3145732
  2.6 1.2 %copy-start.1 = (bf16[1,512,1024]{2,1,0:T(8,128)(2,1)S(1)}, bf16[1,512,1024]{2,1,0:T(8,128)(2,1)}, u32[]{:S(2)}) copy-start(bf16[1,512,1024]{2,1,0:T(8,128)(2,1)} %v_store.1) | copy-start | bytes 3145732
  3.8 0.9 copy-start.2
  4.8 0.9 copy-start.3
  5.7 0.9 copy-start.4
  6.6 0.8 copy-start.5
  7.4 0.8 copy-start.6
  8.2 0.7 copy-start.7
  8.9 0.7 copy-start.8
  9.6 0.7 copy-start.9

commit v2 on v1

v2 whole, which is shorter than its diff:
```python
import functools

import jax
import jax.numpy as jnp
import numpy as np
from jax import lax
from jax.experimental import pallas as pl
from jax.experimental.pallas import tpu as pltpu
from jax.sharding import PartitionSpec as P

HD = 128
PT = 512
RECP = 128
QDEV = 16
PASS = 32
HEADS = 6
ROWS = HEADS * RECP
QROWS = HEADS * QDEV
QSTART = PASS * PT
CHUNK = 512
NP = 2
TOK = 64
VMEM_LIMIT = 62 * 1024 * 1024
FLOOR = -1e30
SCALE = float(np.log2(np.e) / np.sqrt(128.0))
MESH = pl.DeviceIdType.MESH
F32 = jnp.float32
BF16 = jnp.bfloat16

INV_2PI = float(1.0 / (2.0 * np.pi))
PI_A = 6.28125
PI_B = 0.0019350051879882812
PI_C = 3.0199159795074593e-07
SIN_C = [float((-1.0) ** k / np.prod(np.arange(1, 2 * k + 2, dtype=np.float64))) for k in range(9)]
COS_C = [float((-1.0) ** k / np.prod(np.arange(1, 2 * k + 1, dtype=np.float64))) for k in range(10)]


def freq_table():
    half = HD // 2
    freqs = 1000000.0 ** (-np.arange(half, dtype=np.float64) * 2.0 / HD)
    return np.concatenate([freqs, freqs])[None, :].astype(np.float32)


def cos_sin(pos, freq):
    angle = pos * freq
    turns = jnp.floor(angle * INV_2PI + 0.5)
    r = ((angle - turns * PI_A) - turns * PI_B) - turns * PI_C
    r2 = r * r
    s = jnp.full_like(r, SIN_C[8])
    for k in range(7, -1, -1):
        s = s * r2 + SIN_C[k]
    s = s * r
    c = jnp.full_like(r, COS_C[9])
    for k in range(8, -1, -1):
        c = c * r2 + COS_C[k]
    lane = lax.broadcasted_iota(jnp.int32, s.shape, 1)
    return c, jnp.where(lane < HD // 2, -s, s)


def turn(x, c, s):
    return x * c + pltpu.roll(x, HD // 2, 1) * s


def eye_mask(n, m):
    row = lax.broadcasted_iota(jnp.int32, (n, m), 0)
    col = lax.broadcasted_iota(jnp.int32, (n, m), 1)
    return row == col


def to_col(row, n):
    full = jnp.broadcast_to(row, (n, 128))
    return jnp.sum(jnp.where(eye_mask(n, 128), full, 0.0), axis=1, keepdims=True)


def to_row(col, n):
    return jnp.sum(jnp.where(eye_mask(n, 128), col, 0.0), axis=0, keepdims=True)


def nt_dot(a, b):
    return lax.dot_general(a, b, (((1,), (1,)), ((), ())), preferred_element_type=F32)


def kernel(
    pos_off_h, owner_map_h, pids_h, rec_count_h, rec_index_h, freq_h, fresh_q_h, fresh_k_h,
    fresh_v_h, ques_q_h, ques_k_h, ques_v_h, k_store, v_store,
    rec_out, ques_out,
    pos_off, owner_map, pids, rec_count, rec_index, freq_ref, fresh_q, fresh_kv, ques_q, ques_kv,
    xfin0, xfin1, mb00, mb01, mb10, mb11, msend, zsend, zin0, zin1, tab, keep, repl, kall, vall, kq, vq,
    qrec, qques, qpos, mcur, mst, ast, mstq, astq,
    osend, oqsend, orecv, oqrecv, lsend, lrecv,
    isem, lsem, xs, xr, zs, zr, qs, qr, ps, pr, ns, nr, cs, cr, os_, or_,
):
    xfin = (xfin0, xfin1)
    mbuf = ((mb00, mb01), (mb10, mb11))
    zin = (zin0, zin1)
    bank = lax.axis_index("bank")
    blk = lax.axis_index("blk")
    x = lax.div(bank, 4)
    z_hi = lax.rem(bank, 4)
    zh = lax.div(z_hi, 2)
    b1 = lax.rem(z_hi, 2)
    z_lo = lax.div(blk, 16)
    g = lax.rem(blk, 16)
    y = lax.div(g, 2)
    core = lax.rem(g, 2)
    zc = 2 * z_hi + z_lo
    z4 = 2 * b1 + z_lo
    head = 2 * x + zh

    def dev(xx, zz, gg):
        return (xx * 4 + lax.div(zz, 2), lax.rem(zz, 2) * 16 + gg)

    x_up = dev(lax.rem(x + 1, 4), zc, g)
    x_dn = dev(lax.rem(x + 3, 4), zc, g)
    y_up = dev(x, zc, lax.rem(y + 1, 8) * 2 + core)
    y_dn = dev(x, zc, lax.rem(y + 7, 8) * 2 + core)
    y_up2 = dev(x, zc, lax.rem(y + 2, 8) * 2 + core)
    y_dn2 = dev(x, zc, lax.rem(y + 6, 8) * 2 + core)
    twin = dev(x, zc, y * 2 + 1 - core)

    def z_dev(i):
        return dev(x, lax.rem(zc + i, 8), g)

    def z4_dev(i):
        return dev(x, 4 * zh + lax.rem(z4 + i, 4), g)

    def rcopy(src, dst, ssem, rsem, where):
        return pltpu.make_async_remote_copy(
            src_ref=src, dst_ref=dst, send_sem=ssem, recv_sem=rsem,
            device_id=where, device_id_type=MESH,
        )

    def cols(xx):
        return pl.ds(pl.multiple_of(lax.rem(xx, 4) * 256, 256), 256)

    hcol = pl.ds(pl.multiple_of(head * 128, 128), 128)

    barrier = pltpu.get_barrier_semaphore()
    peers = [x_up, x_dn, y_up, y_dn, y_up2, y_dn2, twin] + [z_dev(i) for i in range(1, 8)]
    for peer in peers:
        pl.semaphore_signal(barrier, inc=1, device_id=peer, device_id_type=MESH)

    moves = [
        (fresh_q_h, fresh_q), (rec_index_h, rec_index), (freq_h, freq_ref), (ques_q_h, ques_q),
        (ques_k_h.at[:, hcol], ques_kv.at[0]), (ques_v_h.at[:, hcol], ques_kv.at[1]),
        (owner_map_h, owner_map), (pids_h, pids), (pos_off_h, pos_off), (rec_count_h, rec_count),
        (fresh_k_h.at[:, cols(x)], fresh_kv.at[0]), (fresh_v_h.at[:, cols(x)], fresh_kv.at[1]),
    ]
    moves = [pltpu.make_async_copy(a, b, isem.at[i]) for i, (a, b) in enumerate(moves)]
    for c in moves:
        c.start()

    stores = (k_store, v_store)
    top = pl.ds(0, 2)
    low = pl.ds(2, 2)

    def toks(part):
        return pl.ds(part * TOK, TOK)

    def x_local(part):
        copies = []
        for kv in range(2):
            st = stores[kv]
            for j, (src, dst) in enumerate((
                (st.at[top, toks(part), cols(x + 1)], mbuf[part][0].at[0, kv]),
                (st.at[low, toks(part), cols(x + 3)], mbuf[part][1].at[0, kv]),
                (st.at[top, toks(part), cols(x)], xfin[part].at[0, kv, 0]),
                (st.at[low, toks(part), cols(x)], xfin[part].at[0, kv, 1]),
            )):
                c = pltpu.make_async_copy(src, dst, lsem.at[part, kv, j])
                c.start()
                copies.append(c)
        return copies

    loc = [x_local(part) for part in range(NP)]
    pl.semaphore_wait(barrier, len(peers))

    def x_relay(part):
        copies = []
        for kv in range(2):
            st = stores[kv]
            copies += [
                rcopy(st.at[top, toks(part), cols(x + 2)], mbuf[part][0].at[1, kv],
                      xs.at[part, 0, kv], xr.at[part, 0, kv], x_up),
                rcopy(st.at[low, toks(part), cols(x + 2)], mbuf[part][1].at[1, kv],
                      xs.at[part, 1, kv], xr.at[part, 1, kv], x_dn),
            ]
        for c in copies:
            c.start()
        return copies

    def x_plain(part):
        copies = []
        for kv in range(2):
            st = stores[kv]
            copies += [
                rcopy(st.at[low, toks(part), cols(x + 1)], xfin[part].at[1, kv, 1],
                      xs.at[part, 2, kv], xr.at[part, 2, kv], x_up),
                rcopy(st.at[top, toks(part), cols(x + 3)], xfin[part].at[2, kv, 0],
                      xs.at[part, 3, kv], xr.at[part, 3, kv], x_dn),
            ]
        for c in copies:
            c.start()
        return copies

    def x_merge(part, relay, owner_x):
        copies = []
        for d in range(2):
            for kv in range(2):
                loc[part][kv * 4 + d].wait()
                relay[kv * 2 + d].wait_recv()
            near = lax.rem(x + (3 if d == 0 else 1), 4)
            pick = jnp.where(owner_x == near, 1, 0)
            msend[part, d] = mbuf[part][d][pick]
            c = rcopy(msend.at[part, d], xfin[part].at[1 + d, :, d],
                      xs.at[part, 4 + d, 0], xr.at[part, 4 + d, 0], x_up if d == 0 else x_dn)
            c.start()
            copies.append(c)
        return copies

    def x_finish(part, plain, merged, owner_x, between):
        for kv in range(2):
            loc[part][kv * 4 + 2].wait()
            loc[part][kv * 4 + 3].wait()
        for c in plain + merged:
            c.wait_recv()
        is_own = owner_x == x
        idx_a = jnp.where(is_own, 0, jnp.where(owner_x == lax.rem(x + 1, 4), 2, 1))
        idx_b = jnp.where(is_own, 0, jnp.where(owner_x == lax.rem(x + 3, 4), 1, 2))
        for kv in range(2):
            for quarter in range(4):
                half = quarter // 2
                idx = idx_a if half == 0 else idx_b
                data = xfin[part][idx, kv, half, quarter % 2].astype(F32)
                for hh in range(2):
                    lanes = slice(hh * 128, (hh + 1) * 128)
                    piece = data[:, lanes]
                    if kv == 0:
                        piece = turn(piece, tab[part, quarter, 0], tab[part, quarter, 1])
                    else:
                        piece = piece * keep[part, quarter]
                    piece = piece + repl[part, quarter, kv, :, lanes]
                    zsend[part, hh, quarter, kv] = piece.astype(BF16)
            if kv == 0 and between is not None:
                between()
        copies = []
        for i in (1, 7, 2, 6, 3, 5, 4):
            t = lax.rem(zc + i, 8)
            c = rcopy(
                zsend.at[part, lax.div(t, 4), lax.rem(t, 4)], zin[part].at[i],
                zs.at[part, i - 1], zr.at[part, i - 1], z_dev(i),
            )
            c.start()
            copies.append(c)
        zin[part][0] = zsend[part, zh, z4]
        return copies

    def z_finish(part, copies):
        for c in copies:
            c.wait_recv()
        rows = pl.ds(pl.multiple_of(g * TOK, TOK), TOK)
        for c in range(2):
            owner_z = lax.rem(lax.div(owner_map[pids[c * 16 + g]], 32), 4)
            idx = lax.rem(zc + 8 - (2 * owner_z + c), 8)
            kall[part, c, rows, :] = zin[part][idx, 0]
            vall[part, c, rows, 0:128] = zin[part][idx, 1]

    def gather_slices(fam, gg):
        if fam < 4:
            rows = pl.ds(pl.multiple_of(gg * TOK, TOK), TOK)
            if fam % 2 == 0:
                return kall.at[fam // 2, :, rows, :]
            return vall.at[fam // 2, :, rows, pl.ds(0, 128)]
        rows = pl.ds(pl.multiple_of(gg * 16, 16), 16)
        if fam == 4:
            return kq.at[rows, :]
        return vq.at[rows, pl.ds(0, 128)]

    def reach(fam):
        return (4, 3) if fam % 2 == 0 else (3, 4)

    def at_y(dy):
        return lax.rem(y + 8 + dy, 8) * 2 + core

    def g_copy(fam, dy, which, hop):
        piece = gather_slices(fam, at_y(dy))
        if which == "up":
            return rcopy(piece, piece, ps.at[fam, hop], pr.at[fam, hop], y_up2 if hop % 2 else y_up)
        if which == "dn":
            return rcopy(piece, piece, ns.at[fam, hop], nr.at[fam, hop], y_dn2 if hop % 2 else y_dn)
        return rcopy(piece, piece, cs.at[fam, hop], cr.at[fam, hop], twin)

    def g_send(fam, dy, which, hop):
        g_copy(fam, dy, which, hop).start()

    def g_arrived(fam, dy, which, hop):
        g_copy(fam, dy, which, hop).wait_recv()

    def g_start(fam):
        for hop in range(2):
            g_send(fam, 0, "up", hop)
            g_send(fam, 0, "dn", hop)
        g_send(fam, 0, "twin", 0)

    def g_first(fam):
        n_up, n_dn = reach(fam)
        g_arrived(fam, -2, "up", 1)
        for hop in range(2, n_up):
            g_send(fam, -2, "up", hop)
        g_arrived(fam, 2, "dn", 1)
        for hop in range(2, n_dn):
            g_send(fam, 2, "dn", hop)
        g_send(fam, -2, "twin", 2)
        g_send(fam, 2, "twin", 6)
        g_arrived(fam, -1, "up", 0)
        g_send(fam, -1, "twin", 1)
        g_arrived(fam, 1, "dn", 0)
        g_send(fam, 1, "twin", 5)

    def g_second(fam):
        n_up, n_dn = reach(fam)
        for d in range(3, n_up + 1):
            g_arrived(fam, -d, "up", d - 1)
            g_send(fam, -d, "twin", d)
        for d in range(3, n_dn + 1):
            g_arrived(fam, d, "dn", d - 1)
            g_send(fam, d, "twin", d if d == 4 else 4 + d)

    def twin_hops(fam):
        n_up, n_dn = reach(fam)
        return [(0, 0)] + [(-d, d) for d in range(1, n_up + 1)] + [
            (d, d if d == 4 else 4 + d) for d in range(1, n_dn + 1)
        ]

    def g_end(fam):
        for dy, hop in twin_hops(fam):
            piece = gather_slices(fam, lax.rem(y + 8 + dy, 8) * 2 + 1 - core)
            rcopy(piece, piece, cs.at[fam, hop], cr.at[fam, hop], twin).wait_recv()

    def g_sent(fam):
        n_up, n_dn = reach(fam)
        for hop in range(n_up):
            g_copy(fam, 0 if hop < 2 else -2, "up", hop).wait_send()
        for hop in range(n_dn):
            g_copy(fam, 0 if hop < 2 else 2, "dn", hop).wait_send()
        for dy, hop in twin_hops(fam):
            g_copy(fam, dy, "twin", hop).wait_send()

    relay0 = x_relay(0)
    for c in moves:
        c.wait()
    slot = owner_map[pids[blk]]
    owner_x = lax.div(slot, 128)
    off = pos_off[slot]
    count = rec_count[0]

    freq = freq_ref[...]
    rec_row = rec_index[...].astype(F32)
    rec_pos_row = rec_row + (blk * PT).astype(F32)
    rec_pos = to_col(rec_pos_row, 128)
    c_rec, s_rec = cos_sin(rec_pos, freq)

    @pl.loop(0, HEADS)
    def _(hh):
        at = pl.ds(pl.multiple_of(hh * 128, 128), 128)
        q = turn(fresh_q[:, at].astype(F32), c_rec, s_rec) * SCALE
        qrec[z4, at, :] = q.astype(BF16)

    qpos[z4] = jnp.broadcast_to(rec_pos_row, (8, 128))
    for c in relay0:
        c.wait_send()
    plain0 = x_plain(0)
    ques_pos = (
        lax.broadcasted_iota(jnp.int32, (QDEV, 1), 0) + (QSTART + blk * QDEV)
    ).astype(F32)
    c_q, s_q = cos_sin(ques_pos, freq)
    for hh in range(HEADS):
        lanes = slice(hh * 128, (hh + 1) * 128)
        q = turn(ques_q[:, lanes].astype(F32), c_q, s_q) * SCALE
        qques[pl.ds(pl.multiple_of(z4 * QROWS + hh * 16, 16), 16), :] = q.astype(BF16)
    def src_rows(src):
        return pl.ds(pl.multiple_of(src * QROWS, 16), QROWS)

    q_copies = []
    for i in (1, 3, 2):
        for j, ref in enumerate((qrec.at[z4], qques.at[src_rows(z4)], qpos.at[z4])):
            c = rcopy(ref, ref, qs.at[i - 1, j], qr.at[i - 1, j], z4_dev(i))
            c.start()
            q_copies.append(c)

    my_rows = pl.ds(pl.multiple_of(g * 16, 16), 16)
    kq[my_rows, :] = turn(ques_kv[0].astype(F32), c_q, s_q).astype(BF16)
    vq[my_rows, 0:128] = ques_kv[1]
    merged0 = x_merge(0, relay0, owner_x)
    g_start(4)
    g_start(5)

    off_f = off.astype(F32)
    base_f = (blk * PT).astype(F32)
    slot_lane = lax.broadcasted_iota(jnp.int32, (TOK, 128), 1)

    def tables(part):
        @pl.loop(0, 4)
        def _(quarter):
            first = quarter * 128 + part * TOK
            tok = lax.broadcasted_iota(jnp.int32, (TOK, 128), 0) + first
            match = (tok.astype(F32) == jnp.broadcast_to(rec_row, (TOK, 128))) & (slot_lane < count)
            onehot = jnp.where(match, 1.0, 0.0)
            found = jnp.sum(onehot, axis=1, keepdims=True) > 0.5
            onehot = onehot.astype(BF16)
            tpos = (lax.broadcasted_iota(jnp.int32, (TOK, 1), 0) + first).astype(F32) + base_f
            tpos = tpos - jnp.where(found, 0.0, off_f)
            c_t, s_t = cos_sin(tpos, freq)
            rk = jnp.dot(onehot, fresh_kv[0], preferred_element_type=F32)
            for hh in range(2):
                lanes = slice(hh * 128, (hh + 1) * 128)
                repl[part, quarter, 0, :, lanes] = turn(rk[:, lanes], c_t, s_t)
            repl[part, quarter, 1] = jnp.dot(onehot, fresh_kv[1], preferred_element_type=F32)
            stay = jnp.broadcast_to(jnp.where(found, 0.0, 1.0), (TOK, 128))
            keep[part, quarter] = stay
            tab[part, quarter, 0] = c_t * stay
            tab[part, quarter, 1] = s_t * stay

    tables(0)
    vall[:, :, :, 128:256] = jnp.ones((NP, 2, 16 * TOK, 128), BF16)
    vq[:, 128:256] = jnp.ones((256, 128), BF16)
    for c in merged0:
        c.wait_send()
    relay1 = x_relay(1)
    tables(1)
    plain1 = []

    def go_plain1():
        for c in relay1:
            c.wait_send()
        plain1.extend(x_plain(1))

    z0 = x_finish(0, plain0, merged0, owner_x, go_plain1)
    merged1 = x_merge(1, relay1, owner_x)
    for step in (g_first, g_second):
        step(4)
        step(5)
    z_finish(0, z0)
    g_start(0)
    g_start(1)
    z1 = x_finish(1, plain1, merged1, owner_x, None)
    for step in (g_first, g_second):
        step(0)
        step(1)
    z_finish(1, z1)
    g_start(2)
    g_start(3)
    for fam in (4, 5, 0, 1):
        g_end(fam)
    for c in q_copies:
        c.wait_recv()

    key_lane = lax.broadcasted_iota(jnp.int32, (1, CHUNK), 1)
    key_off = lax.div(key_lane, TOK) * PT + lax.rem(key_lane, TOK) + z4 * 128
    key_off = key_off.astype(F32)

    def chunk_rows(ch):
        return pl.ds(pl.multiple_of(lax.rem(ch, 2) * CHUNK, CHUNK), CHUNK)

    def k_chunk(part, ch):
        return kall[part, lax.div(ch, 2), chunk_rows(ch), :]

    def v_chunk(part, ch):
        return vall[part, lax.div(ch, 2), chunk_rows(ch), :]

    def fold(s):
        m = s[:, 0:128]
        for j in range(1, s.shape[1] // 128):
            m = jnp.maximum(m, s[:, j * 128:(j + 1) * 128])
        return m

    def wide(m, n):
        return jnp.concatenate([m] * (n // 128), axis=1)

    def blocks(n):
        return [(b, slice(b * 128, (b + 1) * 128)) for b in range(n)]

    def attend(n, q_of, open_chunks, keys, values, closing, first, m_ref, a_ref):
        for b, rows in blocks(n):
            mcur[rows, :] = jnp.full((128, 128), FLOOR, F32) if first else m_ref[rows, :]

        @pl.loop(0, open_chunks)
        def _(ch):
            k = keys(ch)
            for b, rows in blocks(n):
                mcur[rows, :] = jnp.maximum(mcur[rows, :], fold(nt_dot(q_of(rows), k)))

        if closing is not None:
            k_last, v_last, mask = closing
            for b, rows in blocks(n):
                s = jnp.where(mask(rows), nt_dot(q_of(rows), k_last()), FLOOR)
                mcur[rows, :] = jnp.maximum(mcur[rows, :], fold(s))
        for b, rows in blocks(n):
            m = jnp.broadcast_to(jnp.max(mcur[rows, :], axis=1, keepdims=True), (128, 128))
            if first:
                a_ref[rows, :] = jnp.zeros((128, 256), F32)
            else:
                a_ref[rows, :] = a_ref[rows, :] * wide(jnp.exp2(m_ref[rows, :] - m), 256)
            m_ref[rows, :] = m

        def add(rows, s, v):
            p = jnp.exp2(s - wide(m_ref[rows, :], s.shape[1])).astype(BF16)
            a_ref[rows, :] = a_ref[rows, :] + jnp.dot(p, v, preferred_element_type=F32)

        @pl.loop(0, open_chunks)
        def _(ch):
            k = keys(ch)
            v = values(ch)
            for b, rows in blocks(n):
                add(rows, nt_dot(q_of(rows), k), v)

        if closing is not None:
            for b, rows in blocks(n):
                add(rows, jnp.where(mask(rows), nt_dot(q_of(rows), k_last()), FLOOR), v_last())

    def log_sum(m, total, n):
        return to_row(m, n) + jnp.log2(jnp.maximum(to_row(total, n), 1e-30))

    lsend[...] = jnp.zeros((4, 8, 128), F32)

    def out_copy(i, j):
        src = lax.rem(z4 + i, 4)
        a, b = (
            (osend.at[i], orecv.at[z4]),
            (oqsend.at[src_rows(src)], oqrecv.at[z4]),
            (lsend.at[src], lrecv.at[z4]),
        )[j]
        return rcopy(a, b, os_.at[i, j], or_.at[i, j], z4_dev(i))

    def ques_mask(rows):
        row = lax.broadcasted_iota(jnp.int32, (128, 1), 0) + rows.start
        row_pos = lax.rem(lax.div(row, QROWS), 2) * 256 + g * 16 + lax.rem(row, 16)
        col = lax.broadcasted_iota(jnp.int32, (1, 256), 1)
        col_mine = lax.div(lax.rem(col, 16), 8) == b1
        return jnp.where(col_mine, z_lo * 256 + col, 100000) <= row_pos

    def ques_pass(part):
        closing = (lambda: kq[...], lambda: vq[...], ques_mask) if part == 0 else None
        attend(
            3, lambda rows: qques[rows, :], 4, lambda ch: k_chunk(part, ch),
            lambda ch: v_chunk(part, ch), closing, part == 0, mstq, astq,
        )
        if part < NP - 1:
            return
        for src in range(4):
            rows = slice(src * QROWS, (src + 1) * QROWS)
            total = astq[rows, 128:256]
            oqsend[rows, :] = (astq[rows, 0:128] / total).astype(BF16)
            lsend[src, 6:7, :] = log_sum(mstq[rows, :], total, QROWS)
        oqrecv[z4] = oqsend[src_rows(z4), :]
        for i in range(1, 4):
            out_copy(i, 1).start()

    def rec_pass(part, i):
        src = lax.rem(z4 + i, 4)
        n_open = 2 * lax.rem(src, 2) + lax.div(g, 8)
        pos_col = to_col(qpos[src, 0:1, :], 128)
        key_pos = key_off + (n_open * (8 * PT) + part * TOK).astype(F32)
        closing = (
            lambda: k_chunk(part, n_open), lambda: v_chunk(part, n_open),
            lambda rows: key_pos <= pos_col,
        )
        m_ref, a_ref = mst.at[i], ast.at[i]
        attend(
            HEADS, lambda rows: qrec[src, rows, :], n_open, lambda ch: k_chunk(part, ch),
            lambda ch: v_chunk(part, ch), closing, part == 0, m_ref, a_ref,
        )
        if part < NP - 1:
            return
        for hh in range(HEADS):
            rows = slice(hh * 128, (hh + 1) * 128)
            total = a_ref[rows, 128:256]
            osend[i, rows, :] = (a_ref[rows, 0:128] / total).astype(BF16)
            lsend[src, hh:hh + 1, :] = log_sum(m_ref[rows, :], total, 128)

        @pl.when(i == 0)
        def _():
            orecv[z4] = osend[0]
            lrecv[z4] = lsend[z4]

        @pl.when(i > 0)
        def _():
            out_copy(i, 0).start()
            out_copy(i, 2).start()

    ques_pass(0)

    @pl.loop(0, 4)
    def _(it):
        @pl.when(it == 1)
        def _():
            g_first(2)
            g_first(3)

        @pl.when(it == 3)
        def _():
            g_second(2)
            g_second(3)

        rec_pass(0, lax.rem(it + 1, 4))

    g_end(2)
    g_end(3)
    ques_pass(1)

    @pl.loop(0, 4)
    def _(it):
        rec_pass(1, lax.rem(it + 1, 4))

    out_copies = [out_copy(i, j) for i in range(1, 4) for j in range(3)]
    for c in out_copies:
        c.wait_recv()

    def join(parts, lses, n):
        cols_ = [to_col(l, n) for l in lses]
        top_ = functools.reduce(jnp.maximum, cols_)
        ws = [jnp.exp2(c - top_) for c in cols_]
        total = ws[0] + ws[1] + ws[2] + ws[3]
        acc = ws[0] * parts[0].astype(F32)
        for w, part in zip(ws[1:], parts[1:]):
            acc = acc + w * part.astype(F32)
        return acc / total

    used = lax.broadcasted_iota(jnp.int32, (128, 1), 0) < count

    @pl.loop(0, HEADS)
    def _(hh):
        rows = pl.ds(pl.multiple_of(hh * 128, 128), 128)
        o = join([orecv[j, rows, :] for j in range(4)], [lrecv[j, pl.ds(hh, 1), :] for j in range(4)], 128)
        rec_out[:, rows] = jnp.where(used, o, 0.0).astype(BF16)

    o = join([oqrecv[j] for j in range(4)], [lrecv[j, 6:7, :] for j in range(4)], QROWS)
    for hh in range(HEADS):
        ques_out[:, hh * 128:(hh + 1) * 128] = o[hh * 16:(hh + 1) * 16].astype(BF16)

    for c in plain0 + plain1 + merged1 + z0 + z1 + q_copies + out_copies:
        c.wait_send()
    for fam in range(6):
        g_sent(fam)


def on_device(
    k_store, v_store, pos_offset, owner_map, passage_ids, rec_index, rec_count,
    fresh_q, fresh_k, fresh_v, ques_q, ques_k, ques_v,
):
    vmem = pl.BlockSpec(memory_space=pltpu.VMEM)
    anym = pl.BlockSpec(memory_space=pl.ANY)
    dma = pltpu.SemaphoreType.DMA
    v = pltpu.VMEM
    smem = pltpu.SMEM
    i32 = jnp.int32
    return pl.pallas_call(
        kernel,
        out_shape=(
            jax.ShapeDtypeStruct((RECP, HEADS * HD), BF16),
            jax.ShapeDtypeStruct((QDEV, HEADS * HD), BF16),
        ),
        in_specs=[anym] * 14,
        out_specs=(vmem, vmem),
        scratch_shapes=[
            smem((512,), i32), smem((512,), i32), smem((32,), i32), smem((1,), i32),
            v((1, 128), i32), v((1, 128), F32), v((RECP, HEADS * HD), BF16),
            v((2, RECP, 256), BF16), v((QDEV, HEADS * HD), BF16), v((2, QDEV, 128), BF16),
            v((3, 2, 2, 2, TOK, 256), BF16), v((3, 2, 2, 2, TOK, 256), BF16),
            v((2, 2, 2, TOK, 256), BF16), v((2, 2, 2, TOK, 256), BF16),
            v((2, 2, 2, TOK, 256), BF16), v((2, 2, 2, TOK, 256), BF16),
            v((NP, 2, 2, 2, TOK, 256), BF16),
            v((NP, 2, 4, 2, TOK, 128), BF16),
            v((8, 2, TOK, 128), BF16), v((8, 2, TOK, 128), BF16),
            v((NP, 4, 2, TOK, 128), F32),
            v((NP, 4, TOK, 128), F32),
            v((NP, 4, 2, TOK, 256), F32),
            v((NP, 2, 16 * TOK, 128), BF16),
            v((NP, 2, 16 * TOK, 256), BF16),
            v((256, 128), BF16),
            v((256, 256), BF16),
            v((4, ROWS, 128), BF16),
            v((4 * QROWS, 128), BF16),
            v((4, 8, 128), F32),
            v((ROWS, 128), F32),
            v((4, ROWS, 128), F32), v((4, ROWS, 256), F32),
            v((4 * QROWS, 128), F32), v((4 * QROWS, 256), F32),
            v((4, ROWS, 128), BF16),
            v((4 * QROWS, 128), BF16),
            v((4, ROWS, 128), BF16),
            v((4, QROWS, 128), BF16),
            v((4, 8, 128), F32),
            v((4, 8, 128), F32),
            dma((12,)),
            dma((NP, 2, 4)),
            dma((NP, 6, 2)), dma((NP, 6, 2)),
            dma((NP, 7)), dma((NP, 7)),
            dma((3, 3)), dma((3, 3)),
            dma((6, 4)), dma((6, 4)),
            dma((6, 4)), dma((6, 4)),
            dma((6, 8)), dma((6, 8)),
            dma((4, 3)), dma((4, 3)),
        ],
        compiler_params=pltpu.CompilerParams(
            collective_id=0, has_side_effects=True, vmem_limit_bytes=VMEM_LIMIT
        ),
        cost_estimate=pl.CostEstimate(
            flops=8_000_000_000, bytes_accessed=4_000_000, transcendentals=15_000_000
        ),
        name="blend_attend",
    )(
        pos_offset, owner_map, passage_ids, rec_count, rec_index, jnp.asarray(freq_table()),
        fresh_q, fresh_k, fresh_v, ques_q, ques_k, ques_v,
        k_store.reshape(4, 128, 1024), v_store.reshape(4, 128, 1024),
    )


def solution(mesh):
    return jax.shard_map(
        on_device,
        mesh=mesh,
        in_specs=(
            P(("bank", "blk"), None, None),
            P(("bank", "blk"), None, None),
            P(),
            P(),
            P(),
            P("blk", None),
            P("blk"),
            P("blk", "bank"),
            P("blk", None),
            P("blk", None),
            P("blk", "bank"),
            P("blk", None),
            P("blk", None),
        ),
        out_specs=(P("blk", "bank"), P("blk", "bank")),
        check_vma=False,
    )
```

time: 114 us -> 106 us (0.930)
  the two profiles are of different devices: /device:TPU:56 before, /device:TPU:115 now
where the time goes in v2:
time: 106 us
  Pallas kernels  102 us (96%)
  local copies, waits for them, and re-layouts  2.23 us (2%)
  between operations  1.3 us (1%)
    pallas_call x1, Pallas kernels, on_device(): pl.pallas_call(kernel, out_shape=(jax.ShapeDtypeStruct((RECP, HEADS * HD)...  102 us
    unnamed x4, local copies, waits for them, and re-layouts  2.23 us

profile of v2, /device:TPU:115, one launch (start us, length us, event | category | flops | bytes accessed | tf_op | source)
XLA Modules:
  0.0 105.5 jit_solution(673159017804647163)
XLA Ops:
  1.3 102.0 %blend_attend.1 = (bf16[128,768]{1,0:T(8,128)(2,1)}, bf16[16,768]{1,0:T(8,128)(2,1)}) custom-call(s32[512]{0:T(512)} %pos_off_h.1, s32[512]{0:T(512)} %owner_map_h.1, s32[32]{0:T(128)} %pids_h.1, s32[1]{0:T(128)S(6)} %copy.18.rec_count_h, s32[1,128]{1,0:T(1,128)} %rec_index_h.1, f32[1,128]{1,0:T(1,128)} %constant.2.clone.freq_h, bf16[128,768]{1,0:T(8,128)(2,1)} %fresh_q_h.1, ...), custom_call_target="tpu_custom_call" | custom-call | flops 8000000000 | bytes 4000000 | tf_op jit(solution)/shard_map/blend_attend/pallas_call | solution.py:657
  103.3 0.0 copy-start
  103.3 1.6 %copy.19 = bf16[128,768]{1,0:T(8,128)(2,1)} copy(bf16[128,768]{1,0:T(8,128)(2,1)} %get-tuple-element.4) | data formatting | bytes 393216
  104.9 0.0 copy-done
  104.9 0.6 copy.20
Async XLA Ops:
  103.3 1.6 %copy-start = (bf16[16,768]{1,0:T(8,128)(2,1)S(1)}, bf16[16,768]{1,0:T(8,128)(2,1)}, u32[]{:S(2)}) copy-start(bf16[16,768]{1,0:T(8,128)(2,1)} %get-tuple-element.5) | copy-start | bytes 73732

commit v3 on v2

--- a/solution.py
+++ b/solution.py
@@ -22,7 +22,7 @@
 TOK = 64
 VMEM_LIMIT = 62 * 1024 * 1024
 FLOOR = -1e30
-SCALE = float(np.log2(np.e) / np.sqrt(128.0))
+SCALE = float(1.0 / np.sqrt(128.0))
 MESH = pl.DeviceIdType.MESH
 F32 = jnp.float32
 BF16 = jnp.bfloat16
@@ -85,9 +85,9 @@
     fresh_v_h, ques_q_h, ques_k_h, ques_v_h, k_store, v_store,
     rec_out, ques_out,
     pos_off, owner_map, pids, rec_count, rec_index, freq_ref, fresh_q, fresh_kv, ques_q, ques_kv,
-    xfin0, xfin1, mb00, mb01, mb10, mb11, msend, zsend, zin0, zin1, tab, keep, repl, kall, vall, kq, vq,
-    qrec, qques, qpos, mcur, mst, ast, mstq, astq,
-    osend, oqsend, orecv, oqrecv, lsend, lrecv,
+    xfin0, xfin1, mb00, mb01, mb10, mb11, msend, zsend, zin0, zin1, tab, keep, repl, kvall, kvq,
+    qall, qpos, kt, mst, ast,
+    osend, orecv, lsend, lrecv,
     isem, lsem, xs, xr, zs, zr, qs, qr, ps, pr, ns, nr, cs, cr, os_, or_,
 ):
     xfin = (xfin0, xfin1)
@@ -106,6 +106,7 @@
     zc = 2 * z_hi + z_lo
     z4 = 2 * b1 + z_lo
     head = 2 * x + zh
+    w = 2 * z_lo + b1
 
     def dev(xx, zz, gg):
         return (xx * 4 + lax.div(zz, 2), lax.rem(zz, 2) * 16 + gg)
@@ -121,8 +122,10 @@
     def z_dev(i):
         return dev(x, lax.rem(zc + i, 8), g)
 
-    def z4_dev(i):
-        return dev(x, 4 * zh + lax.rem(z4 + i, 4), g)
+    def peer_of(j):
+        b = b1 if j == 0 else 1 - b1
+        lo = z_lo if j == 2 else 1 - z_lo
+        return 2 * lo + b, dev(x, 4 * zh + 2 * b + lo, g)
 
     def rcopy(src, dst, ssem, rsem, where):
         return pltpu.make_async_remote_copy(
@@ -262,19 +265,13 @@
         for c in range(2):
             owner_z = lax.rem(lax.div(owner_map[pids[c * 16 + g]], 32), 4)
             idx = lax.rem(zc + 8 - (2 * owner_z + c), 8)
-            kall[part, c, rows, :] = zin[part][idx, 0]
-            vall[part, c, rows, 0:128] = zin[part][idx, 1]
+            kvall[part, 0, c, rows, :] = zin[part][idx, 0]
+            kvall[part, 1, c, rows, :] = zin[part][idx, 1]
 
     def gather_slices(fam, gg):
-        if fam < 4:
-            rows = pl.ds(pl.multiple_of(gg * TOK, TOK), TOK)
-            if fam % 2 == 0:
-                return kall.at[fam // 2, :, rows, :]
-            return vall.at[fam // 2, :, rows, pl.ds(0, 128)]
-        rows = pl.ds(pl.multiple_of(gg * 16, 16), 16)
-        if fam == 4:
-            return kq.at[rows, :]
-        return vq.at[rows, pl.ds(0, 128)]
+        if fam < 2:
+            return kvall.at[fam, :, :, pl.ds(pl.multiple_of(gg * TOK, TOK), TOK), :]
+        return kvq.at[:, pl.ds(pl.multiple_of(gg * 16, 16), 16), :]
 
     def reach(fam):
         return (4, 3) if fam % 2 == 0 else (3, 4)
@@ -364,9 +361,9 @@
     def _(hh):
         at = pl.ds(pl.multiple_of(hh * 128, 128), 128)
         q = turn(fresh_q[:, at].astype(F32), c_rec, s_rec) * SCALE
-        qrec[z4, at, :] = q.astype(BF16)
-
-    qpos[z4] = jnp.broadcast_to(rec_pos_row, (8, 128))
+        qall[w, at, :] = q.astype(BF16)
+
+    qpos[w] = jnp.broadcast_to(rec_pos_row, (8, 128))
     for c in relay0:
         c.wait_send()
     plain0 = x_plain(0)
@@ -377,23 +374,19 @@
     for hh in range(HEADS):
         lanes = slice(hh * 128, (hh + 1) * 128)
         q = turn(ques_q[:, lanes].astype(F32), c_q, s_q) * SCALE
-        qques[pl.ds(pl.multiple_of(z4 * QROWS + hh * 16, 16), 16), :] = q.astype(BF16)
-    def src_rows(src):
-        return pl.ds(pl.multiple_of(src * QROWS, 16), QROWS)
-
+        qall[w, ROWS + hh * 16:ROWS + (hh + 1) * 16, :] = q.astype(BF16)
     q_copies = []
-    for i in (1, 3, 2):
-        for j, ref in enumerate((qrec.at[z4], qques.at[src_rows(z4)], qpos.at[z4])):
-            c = rcopy(ref, ref, qs.at[i - 1, j], qr.at[i - 1, j], z4_dev(i))
+    for j in range(3):
+        for n, ref in enumerate((qall, qpos)):
+            c = rcopy(ref.at[w], ref.at[w], qs.at[j, n], qr.at[j, n], peer_of(j)[1])
             c.start()
             q_copies.append(c)
 
     my_rows = pl.ds(pl.multiple_of(g * 16, 16), 16)
-    kq[my_rows, :] = turn(ques_kv[0].astype(F32), c_q, s_q).astype(BF16)
-    vq[my_rows, 0:128] = ques_kv[1]
+    kvq[0, my_rows, :] = turn(ques_kv[0].astype(F32), c_q, s_q).astype(BF16)
+    kvq[1, my_rows, :] = ques_kv[1]
     merged0 = x_merge(0, relay0, owner_x)
-    g_start(4)
-    g_start(5)
+    g_start(2)
 
     off_f = off.astype(F32)
     base_f = (blk * PT).astype(F32)
@@ -422,8 +415,6 @@
             tab[part, quarter, 1] = s_t * stay
 
     tables(0)
-    vall[:, :, :, 128:256] = jnp.ones((NP, 2, 16 * TOK, 128), BF16)
-    vq[:, 128:256] = jnp.ones((256, 128), BF16)
     for c in merged0:
         c.wait_send()
     relay1 = x_relay(1)
@@ -437,21 +428,17 @@
 
     z0 = x_finish(0, plain0, merged0, owner_x, go_plain1)
     merged1 = x_merge(1, relay1, owner_x)
-    for step in (g_first, g_second):
-        step(4)
-        step(5)
+    g_first(2)
+    g_second(2)
     z_finish(0, z0)
     g_start(0)
+    z1 = x_finish(1, plain1, merged1, owner_x, None)
+    g_first(0)
+    g_second(0)
+    z_finish(1, z1)
     g_start(1)
-    z1 = x_finish(1, plain1, merged1, owner_x, None)
-    for step in (g_first, g_second):
-        step(0)
-        step(1)
-    z_finish(1, z1)
-    g_start(2)
-    g_start(3)
-    for fam in (4, 5, 0, 1):
-        g_end(fam)
+    g_end(2)
+    g_end(0)
     for c in q_copies:
         c.wait_recv()
 
@@ -462,11 +449,15 @@
     def chunk_rows(ch):
         return pl.ds(pl.multiple_of(lax.rem(ch, 2) * CHUNK, CHUNK), CHUNK)
 
-    def k_chunk(part, ch):
-        return kall[part, lax.div(ch, 2), chunk_rows(ch), :]
+    ones = jnp.ones((CHUNK, 128), BF16)
+
+    def transpose_keys(part):
+        @pl.loop(0, 4)
+        def _(ch):
+            kt[ch] = jnp.transpose(kvall[part, 0, lax.div(ch, 2), chunk_rows(ch), :])
 
     def v_chunk(part, ch):
-        return vall[part, lax.div(ch, 2), chunk_rows(ch), :]
+        return jnp.concatenate([kvall[part, 1, lax.div(ch, 2), chunk_rows(ch), :], ones], axis=1)
 
     def fold(s):
         m = s[:, 0:128]
@@ -477,149 +468,147 @@
     def wide(m, n):
         return jnp.concatenate([m] * (n // 128), axis=1)
 
-    def blocks(n):
-        return [(b, slice(b * 128, (b + 1) * 128)) for b in range(n)]
-
-    def attend(n, q_of, open_chunks, keys, values, closing, first, m_ref, a_ref):
-        for b, rows in blocks(n):
-            mcur[rows, :] = jnp.full((128, 128), FLOOR, F32) if first else m_ref[rows, :]
+    def attend(n, rows_each, q_of, part, open_chunks, closing, m_ref, a_ref):
+        blocks = [(b, slice(b * rows_each, (b + 1) * rows_each)) for b in range(n)]
+        when, last_keys, last_values, mask = closing
+
+        def step(b, rows, k, v, seen):
+            s = jnp.dot(q_of(b), k, preferred_element_type=F32)
+            if seen is not None:
+                s = jnp.where(seen, s, FLOOR)
+            old = m_ref[rows, :]
+            new = jnp.maximum(old, jnp.max(fold(s), axis=1, keepdims=True))
+            m_ref[rows, :] = new
+            p = jnp.exp(s - wide(new, s.shape[1])).astype(BF16)
+            scale = wide(jnp.exp(old - new), 256)
+            a_ref[rows, :] = a_ref[rows, :] * scale + jnp.dot(p, v, preferred_element_type=F32)
 
         @pl.loop(0, open_chunks)
         def _(ch):
-            k = keys(ch)
-            for b, rows in blocks(n):
-                mcur[rows, :] = jnp.maximum(mcur[rows, :], fold(nt_dot(q_of(rows), k)))
-
-        if closing is not None:
-            k_last, v_last, mask = closing
-            for b, rows in blocks(n):
-                s = jnp.where(mask(rows), nt_dot(q_of(rows), k_last()), FLOOR)
-                mcur[rows, :] = jnp.maximum(mcur[rows, :], fold(s))
-        for b, rows in blocks(n):
-            m = jnp.broadcast_to(jnp.max(mcur[rows, :], axis=1, keepdims=True), (128, 128))
-            if first:
-                a_ref[rows, :] = jnp.zeros((128, 256), F32)
-            else:
-                a_ref[rows, :] = a_ref[rows, :] * wide(jnp.exp2(m_ref[rows, :] - m), 256)
-            m_ref[rows, :] = m
-
-        def add(rows, s, v):
-            p = jnp.exp2(s - wide(m_ref[rows, :], s.shape[1])).astype(BF16)
-            a_ref[rows, :] = a_ref[rows, :] + jnp.dot(p, v, preferred_element_type=F32)
-
-        @pl.loop(0, open_chunks)
-        def _(ch):
-            k = keys(ch)
-            v = values(ch)
-            for b, rows in blocks(n):
-                add(rows, nt_dot(q_of(rows), k), v)
-
-        if closing is not None:
-            for b, rows in blocks(n):
-                add(rows, jnp.where(mask(rows), nt_dot(q_of(rows), k_last()), FLOOR), v_last())
+            k = kt[ch]
+            v = v_chunk(part, ch)
+            for b, rows in blocks:
+                step(b, rows, k, v, None)
+
+        def close():
+            k = last_keys()
+            v = last_values()
+            seen = mask()
+            for b, rows in blocks:
+                step(b, rows, k, v, seen)
+
+        if when is None:
+            close()
+        else:
+            pl.when(when)(close)
 
     def log_sum(m, total, n):
-        return to_row(m, n) + jnp.log2(jnp.maximum(to_row(total, n), 1e-30))
+        return to_row(m, n) + jnp.log(jnp.maximum(to_row(total, n), 1e-30))
 
     lsend[...] = jnp.zeros((4, 8, 128), F32)
-
-    def out_copy(i, j):
-        src = lax.rem(z4 + i, 4)
-        a, b = (
-            (osend.at[i], orecv.at[z4]),
-            (oqsend.at[src_rows(src)], oqrecv.at[z4]),
-            (lsend.at[src], lrecv.at[z4]),
-        )[j]
-        return rcopy(a, b, os_.at[i, j], or_.at[i, j], z4_dev(i))
-
-    def ques_mask(rows):
-        row = lax.broadcasted_iota(jnp.int32, (128, 1), 0) + rows.start
-        row_pos = lax.rem(lax.div(row, QROWS), 2) * 256 + g * 16 + lax.rem(row, 16)
+    mst[...] = jnp.full((3, 2 * ROWS, 128), FLOOR, F32)
+    ast[...] = jnp.zeros((3, 2 * ROWS, 256), F32)
+
+    def out_copy(j, n):
+        to, where = peer_of(j)
+        a, b = ((osend, orecv), (lsend, lrecv))[n]
+        return rcopy(a.at[to], b.at[w], os_.at[j, n], or_.at[j, n], where)
+
+    def ques_mask():
+        row = lax.broadcasted_iota(jnp.int32, (4 * QROWS, 1), 0)
+        row_pos = lax.div(row, 2 * QROWS) * 256 + g * 16 + lax.rem(row, 16)
         col = lax.broadcasted_iota(jnp.int32, (1, 256), 1)
         col_mine = lax.div(lax.rem(col, 16), 8) == b1
         return jnp.where(col_mine, z_lo * 256 + col, 100000) <= row_pos
 
     def ques_pass(part):
-        closing = (lambda: kq[...], lambda: vq[...], ques_mask) if part == 0 else None
+        closing = (
+            part == 0, lambda: jnp.transpose(kvq[0]),
+            lambda: jnp.concatenate([kvq[1], ones[0:256]], axis=1), ques_mask,
+        )
         attend(
-            3, lambda rows: qques[rows, :], 4, lambda ch: k_chunk(part, ch),
-            lambda ch: v_chunk(part, ch), closing, part == 0, mstq, astq,
+            1, 4 * QROWS, lambda b: jnp.concatenate([qall[j, ROWS:, :] for j in range(4)], axis=0),
+            part, 4, closing, mst.at[2], ast.at[2],
         )
-        if part < NP - 1:
-            return
-        for src in range(4):
-            rows = slice(src * QROWS, (src + 1) * QROWS)
-            total = astq[rows, 128:256]
-            oqsend[rows, :] = (astq[rows, 0:128] / total).astype(BF16)
-            lsend[src, 6:7, :] = log_sum(mstq[rows, :], total, QROWS)
-        oqrecv[z4] = oqsend[src_rows(z4), :]
-        for i in range(1, 4):
-            out_copy(i, 1).start()
-
-    def rec_pass(part, i):
-        src = lax.rem(z4 + i, 4)
-        n_open = 2 * lax.rem(src, 2) + lax.div(g, 8)
-        pos_col = to_col(qpos[src, 0:1, :], 128)
+
+        @pl.when(part == NP - 1)
+        def _():
+            for src in range(4):
+                rows = slice(src * QROWS, (src + 1) * QROWS)
+                total = ast[2, rows, 128:256]
+                osend[src, ROWS:, :] = (ast[2, rows, 0:128] / total).astype(BF16)
+                lsend[src, 6:7, :] = log_sum(mst[2, rows, :], total, QROWS)
+
+    def rec_pass(part, c):
+        n_open = 2 * c + lax.div(g, 8)
+        pos_col = to_col(qpos[2 * c, 0:1, :], 128)
+        pos_col = jnp.concatenate([pos_col] * HEADS, axis=0)
         key_pos = key_off + (n_open * (8 * PT) + part * TOK).astype(F32)
         closing = (
-            lambda: k_chunk(part, n_open), lambda: v_chunk(part, n_open),
-            lambda rows: key_pos <= pos_col,
+            None, lambda: kt[n_open], lambda: v_chunk(part, n_open),
+            lambda: key_pos <= pos_col,
         )
-        m_ref, a_ref = mst.at[i], ast.at[i]
         attend(
-            HEADS, lambda rows: qrec[src, rows, :], n_open, lambda ch: k_chunk(part, ch),
-            lambda ch: v_chunk(part, ch), closing, part == 0, m_ref, a_ref,
+            2, ROWS, lambda b: qall[2 * c + b, 0:ROWS, :],
+            part, n_open, closing, mst.at[c], ast.at[c],
         )
-        if part < NP - 1:
-            return
-        for hh in range(HEADS):
-            rows = slice(hh * 128, (hh + 1) * 128)
-            total = a_ref[rows, 128:256]
-            osend[i, rows, :] = (a_ref[rows, 0:128] / total).astype(BF16)
-            lsend[src, hh:hh + 1, :] = log_sum(m_ref[rows, :], total, 128)
-
-        @pl.when(i == 0)
+
+    def rec_end(c):
+        for b in range(2):
+            src = 2 * c + b
+            for hh in range(HEADS):
+                rows = slice(b * ROWS + hh * 128, b * ROWS + (hh + 1) * 128)
+                total = ast[c, rows, 128:256]
+                osend[src, hh * 128:(hh + 1) * 128, :] = (ast[c, rows, 0:128] / total).astype(BF16)
+                lsend[src, hh:hh + 1, :] = log_sum(mst[c, rows, :], total, 128)
+
+    @pl.loop(0, NP)
+    def _(part):
+        transpose_keys(part)
+        ques_pass(part)
+
+        @pl.loop(0, 2)
+        def _(t):
+            @pl.when((part == 0) & (t == 0))
+            def _():
+                g_first(1)
+
+            @pl.when((part == 0) & (t == 1))
+            def _():
+                g_second(1)
+
+            c = lax.rem(z_lo + 1 + t, 2)
+            rec_pass(part, c)
+
+            @pl.when(part == NP - 1)
+            def _():
+                rec_end(c)
+
+            @pl.when((part == NP - 1) & (t == 0))
+            def _():
+                for j in range(2):
+                    for n in range(2):
+                        out_copy(j, n).start()
+
+            @pl.when((part == NP - 1) & (t == 1))
+            def _():
+                for n in range(2):
+                    out_copy(2, n).start()
+
+        @pl.when(part == 0)
         def _():
-            orecv[z4] = osend[0]
-            lrecv[z4] = lsend[z4]
-
-        @pl.when(i > 0)
-        def _():
-            out_copy(i, 0).start()
-            out_copy(i, 2).start()
-
-    ques_pass(0)
-
-    @pl.loop(0, 4)
-    def _(it):
-        @pl.when(it == 1)
-        def _():
-            g_first(2)
-            g_first(3)
-
-        @pl.when(it == 3)
-        def _():
-            g_second(2)
-            g_second(3)
-
-        rec_pass(0, lax.rem(it + 1, 4))
-
-    g_end(2)
-    g_end(3)
-    ques_pass(1)
-
-    @pl.loop(0, 4)
-    def _(it):
-        rec_pass(1, lax.rem(it + 1, 4))
-
-    out_copies = [out_copy(i, j) for i in range(1, 4) for j in range(3)]
+            g_end(1)
+
+    orecv[w] = osend[w]
+    lrecv[w] = lsend[w]
+    out_copies = [out_copy(j, n) for j in range(3) for n in range(2)]
     for c in out_copies:
         c.wait_recv()
 
     def join(parts, lses, n):
         cols_ = [to_col(l, n) for l in lses]
         top_ = functools.reduce(jnp.maximum, cols_)
-        ws = [jnp.exp2(c - top_) for c in cols_]
+        ws = [jnp.exp(c - top_) for c in cols_]
         total = ws[0] + ws[1] + ws[2] + ws[3]
         acc = ws[0] * parts[0].astype(F32)
         for w, part in zip(ws[1:], parts[1:]):
@@ -634,13 +623,13 @@
         o = join([orecv[j, rows, :] for j in range(4)], [lrecv[j, pl.ds(hh, 1), :] for j in range(4)], 128)
         rec_out[:, rows] = jnp.where(used, o, 0.0).astype(BF16)
 
-    o = join([oqrecv[j] for j in range(4)], [lrecv[j, 6:7, :] for j in range(4)], QROWS)
+    o = join([orecv[j, ROWS:, :] for j in range(4)], [lrecv[j, 6:7, :] for j in range(4)], QROWS)
     for hh in range(HEADS):
         ques_out[:, hh * 128:(hh + 1) * 128] = o[hh * 16:(hh + 1) * 16].astype(BF16)
 
     for c in plain0 + plain1 + merged1 + z0 + z1 + q_copies + out_copies:
         c.wait_send()
-    for fam in range(6):
+    for fam in range(3):
         g_sent(fam)
 
 
@@ -675,31 +664,25 @@
             v((NP, 4, 2, TOK, 128), F32),
             v((NP, 4, TOK, 128), F32),
             v((NP, 4, 2, TOK, 256), F32),
-            v((NP, 2, 16 * TOK, 128), BF16),
-            v((NP, 2, 16 * TOK, 256), BF16),
-            v((256, 128), BF16),
-            v((256, 256), BF16),
-            v((4, ROWS, 128), BF16),
-            v((4 * QROWS, 128), BF16),
+            v((NP, 2, 2, 16 * TOK, 128), BF16),
+            v((2, 256, 128), BF16),
+            v((4, ROWS + QROWS, 128), BF16),
             v((4, 8, 128), F32),
-            v((ROWS, 128), F32),
-            v((4, ROWS, 128), F32), v((4, ROWS, 256), F32),
-            v((4 * QROWS, 128), F32), v((4 * QROWS, 256), F32),
-            v((4, ROWS, 128), BF16),
-            v((4 * QROWS, 128), BF16),
-            v((4, ROWS, 128), BF16),
-            v((4, QROWS, 128), BF16),
+            v((4, 128, CHUNK), BF16),
+            v((3, 2 * ROWS, 128), F32), v((3, 2 * ROWS, 256), F32),
+            v((4, ROWS + QROWS, 128), BF16),
+            v((4, ROWS + QROWS, 128), BF16),
             v((4, 8, 128), F32),
             v((4, 8, 128), F32),
             dma((12,)),
             dma((NP, 2, 4)),
             dma((NP, 6, 2)), dma((NP, 6, 2)),
             dma((NP, 7)), dma((NP, 7)),
-            dma((3, 3)), dma((3, 3)),
-            dma((6, 4)), dma((6, 4)),
-            dma((6, 4)), dma((6, 4)),
-            dma((6, 8)), dma((6, 8)),
-            dma((4, 3)), dma((4, 3)),
+            dma((3, 2)), dma((3, 2)),
+            dma((3, 4)), dma((3, 4)),
+            dma((3, 4)), dma((3, 4)),
+            dma((3, 8)), dma((3, 8)),
+            dma((3, 2)), dma((3, 2)),
         ],
         compiler_params=pltpu.CompilerParams(
             collective_id=0, has_side_effects=True, vmem_limit_bytes=VMEM_LIMIT

time: 106 us -> 107 us (level)
  the two profiles are of different devices: /device:TPU:115 before, /device:TPU:56 now
where the time goes in v3:
time: 107 us
  Pallas kernels  103 us (96%)
  local copies, waits for them, and re-layouts  2.23 us (2%)
  between operations  1.3 us (1%)
    pallas_call x1, Pallas kernels, on_device(): pl.pallas_call(kernel, out_shape=(jax.ShapeDtypeStruct((RECP, HEADS * HD)...  103 us
    unnamed x4, local copies, waits for them, and re-layouts  2.23 us

profile of v3, /device:TPU:56, one launch (start us, length us, event | category | flops | bytes accessed | tf_op | source)
XLA Modules:
  0.0 106.6 jit_solution(7371888578117425193)
XLA Ops:
  1.3 103.1 %blend_attend.1 = (bf16[128,768]{1,0:T(8,128)(2,1)}, bf16[16,768]{1,0:T(8,128)(2,1)}) custom-call(s32[512]{0:T(512)} %pos_off_h.1, s32[512]{0:T(512)} %owner_map_h.1, s32[32]{0:T(128)} %pids_h.1, s32[1]{0:T(128)S(6)} %copy.18.rec_count_h, s32[1,128]{1,0:T(1,128)} %rec_index_h.1, f32[1,128]{1,0:T(1,128)} %constant.2.clone.freq_h, bf16[128,768]{1,0:T(8,128)(2,1)} %fresh_q_h.1, ...), custom_call_target="tpu_custom_call" | custom-call | flops 8000000000 | bytes 4000000 | tf_op jit(solution)/shard_map/blend_attend/pallas_call | solution.py:646
  104.4 0.0 copy-start
  104.4 1.6 %copy.19 = bf16[128,768]{1,0:T(8,128)(2,1)} copy(bf16[128,768]{1,0:T(8,128)(2,1)} %get-tuple-element.4) | data formatting | bytes 393216
  106.0 0.0 copy-done
  106.0 0.6 copy.20
Async XLA Ops:
  104.4 1.6 %copy-start = (bf16[16,768]{1,0:T(8,128)(2,1)S(1)}, bf16[16,768]{1,0:T(8,128)(2,1)}, u32[]{:S(2)}) copy-start(bf16[16,768]{1,0:T(8,128)(2,1)} %get-tuple-element.5) | copy-start | bytes 73732

commit v4 on v3

--- a/solution.py
+++ b/solution.py
@@ -88,7 +88,7 @@
     xfin0, xfin1, mb00, mb01, mb10, mb11, msend, zsend, zin0, zin1, tab, keep, repl, kvall, kvq,
     qall, qpos, kt, mst, ast,
     osend, orecv, lsend, lrecv,
-    isem, lsem, xs, xr, zs, zr, qs, qr, ps, pr, ns, nr, cs, cr, os_, or_,
+    isem, lsem, xs, xr, zs, zr, bs, br, qs, qr, ps, pr, ns, nr, cs, cr, os_, or_,
 ):
     xfin = (xfin0, xfin1)
     mbuf = ((mb00, mb01), (mb10, mb11))
@@ -106,7 +106,6 @@
     zc = 2 * z_hi + z_lo
     z4 = 2 * b1 + z_lo
     head = 2 * x + zh
-    w = 2 * z_lo + b1
 
     def dev(xx, zz, gg):
         return (xx * 4 + lax.div(zz, 2), lax.rem(zz, 2) * 16 + gg)
@@ -122,10 +121,8 @@
     def z_dev(i):
         return dev(x, lax.rem(zc + i, 8), g)
 
-    def peer_of(j):
-        b = b1 if j == 0 else 1 - b1
-        lo = z_lo if j == 2 else 1 - z_lo
-        return 2 * lo + b, dev(x, 4 * zh + 2 * b + lo, g)
+    partner = dev(x, 4 * zh + 2 * b1 + 1 - z_lo, g)
+    other_b = dev(x, 4 * zh + 2 * (1 - b1) + z_lo, g)
 
     def rcopy(src, dst, ssem, rsem, where):
         return pltpu.make_async_remote_copy(
@@ -258,19 +255,32 @@
         zin[part][0] = zsend[part, zh, z4]
         return copies
 
+    def g_rows(gg):
+        return pl.ds(pl.multiple_of(gg * TOK, TOK), TOK)
+
+    def swap_copy(part):
+        piece = kvall.at[part, b1, :, :, g_rows(g), :]
+        return rcopy(piece, piece, bs.at[part], br.at[part], other_b)
+
     def z_finish(part, copies):
         for c in copies:
             c.wait_recv()
-        rows = pl.ds(pl.multiple_of(g * TOK, TOK), TOK)
         for c in range(2):
             owner_z = lax.rem(lax.div(owner_map[pids[c * 16 + g]], 32), 4)
             idx = lax.rem(zc + 8 - (2 * owner_z + c), 8)
-            kvall[part, 0, c, rows, :] = zin[part][idx, 0]
-            kvall[part, 1, c, rows, :] = zin[part][idx, 1]
+            kvall[part, b1, 0, c, g_rows(g), :] = zin[part][idx, 0]
+            kvall[part, b1, 1, c, g_rows(g), :] = zin[part][idx, 1]
+        swap_copy(part).start()
+        g_start(2 * part)
+
+    def swap_finish(part):
+        piece = kvall.at[part, 1 - b1, :, :, g_rows(g), :]
+        rcopy(piece, piece, bs.at[part], br.at[part], other_b).wait_recv()
+        g_start(2 * part + 1)
 
     def gather_slices(fam, gg):
-        if fam < 2:
-            return kvall.at[fam, :, :, pl.ds(pl.multiple_of(gg * TOK, TOK), TOK), :]
+        if fam < 4:
+            return kvall.at[fam // 2, b1 if fam % 2 == 0 else 1 - b1, :, :, g_rows(gg), :]
         return kvq.at[:, pl.ds(pl.multiple_of(gg * 16, 16), 16), :]
 
     def reach(fam):
@@ -361,9 +371,9 @@
     def _(hh):
         at = pl.ds(pl.multiple_of(hh * 128, 128), 128)
         q = turn(fresh_q[:, at].astype(F32), c_rec, s_rec) * SCALE
-        qall[w, at, :] = q.astype(BF16)
-
-    qpos[w] = jnp.broadcast_to(rec_pos_row, (8, 128))
+        qall[z_lo, at, :] = q.astype(BF16)
+
+    qpos[z_lo] = jnp.broadcast_to(rec_pos_row, (8, 128))
     for c in relay0:
         c.wait_send()
     plain0 = x_plain(0)
@@ -374,19 +384,18 @@
     for hh in range(HEADS):
         lanes = slice(hh * 128, (hh + 1) * 128)
         q = turn(ques_q[:, lanes].astype(F32), c_q, s_q) * SCALE
-        qall[w, ROWS + hh * 16:ROWS + (hh + 1) * 16, :] = q.astype(BF16)
+        qall[z_lo, ROWS + hh * 16:ROWS + (hh + 1) * 16, :] = q.astype(BF16)
     q_copies = []
-    for j in range(3):
-        for n, ref in enumerate((qall, qpos)):
-            c = rcopy(ref.at[w], ref.at[w], qs.at[j, n], qr.at[j, n], peer_of(j)[1])
-            c.start()
-            q_copies.append(c)
+    for n, ref in enumerate((qall, qpos)):
+        c = rcopy(ref.at[z_lo], ref.at[z_lo], qs.at[n], qr.at[n], partner)
+        c.start()
+        q_copies.append(c)
 
     my_rows = pl.ds(pl.multiple_of(g * 16, 16), 16)
     kvq[0, my_rows, :] = turn(ques_kv[0].astype(F32), c_q, s_q).astype(BF16)
     kvq[1, my_rows, :] = ques_kv[1]
     merged0 = x_merge(0, relay0, owner_x)
-    g_start(2)
+    g_start(4)
 
     off_f = off.astype(F32)
     base_f = (blk * PT).astype(F32)
@@ -428,36 +437,41 @@
 
     z0 = x_finish(0, plain0, merged0, owner_x, go_plain1)
     merged1 = x_merge(1, relay1, owner_x)
-    g_first(2)
-    g_second(2)
+    g_first(4)
+    g_second(4)
     z_finish(0, z0)
-    g_start(0)
+    swap_finish(0)
     z1 = x_finish(1, plain1, merged1, owner_x, None)
-    g_first(0)
-    g_second(0)
+    for step in (g_first, g_second):
+        step(0)
+        step(1)
     z_finish(1, z1)
-    g_start(1)
-    g_end(2)
+    g_end(4)
     g_end(0)
+    g_end(1)
     for c in q_copies:
         c.wait_recv()
-
-    key_lane = lax.broadcasted_iota(jnp.int32, (1, CHUNK), 1)
-    key_off = lax.div(key_lane, TOK) * PT + lax.rem(key_lane, TOK) + z4 * 128
-    key_off = key_off.astype(F32)
-
-    def chunk_rows(ch):
-        return pl.ds(pl.multiple_of(lax.rem(ch, 2) * CHUNK, CHUNK), CHUNK)
-
-    ones = jnp.ones((CHUNK, 128), BF16)
+    swap_finish(1)
+
+    key_lane = lax.broadcasted_iota(jnp.int32, (1, 2 * CHUNK), 1)
+    key_in = lax.rem(key_lane, CHUNK)
+    key_off = lax.div(key_in, TOK) * PT + lax.rem(key_in, TOK)
+    key_off = (key_off + (2 * lax.div(key_lane, CHUNK) + z_lo) * 128).astype(F32)
+    ones = jnp.ones((2 * CHUNK, 128), BF16)
+
+    def chunk_of(part, b, kv, ch):
+        rows = pl.ds(pl.multiple_of(lax.rem(ch, 2) * CHUNK, CHUNK), CHUNK)
+        return kvall[part, b, kv, lax.div(ch, 2), rows, :]
 
     def transpose_keys(part):
         @pl.loop(0, 4)
         def _(ch):
-            kt[ch] = jnp.transpose(kvall[part, 0, lax.div(ch, 2), chunk_rows(ch), :])
+            for b in range(2):
+                kt[ch, :, b * CHUNK:(b + 1) * CHUNK] = jnp.transpose(chunk_of(part, b, 0, ch))
 
     def v_chunk(part, ch):
-        return jnp.concatenate([kvall[part, 1, lax.div(ch, 2), chunk_rows(ch), :], ones], axis=1)
+        v = jnp.concatenate([chunk_of(part, b, 1, ch) for b in range(2)], axis=0)
+        return jnp.concatenate([v, ones], axis=1)
 
     def fold(s):
         m = s[:, 0:128]
@@ -505,21 +519,19 @@
     def log_sum(m, total, n):
         return to_row(m, n) + jnp.log(jnp.maximum(to_row(total, n), 1e-30))
 
-    lsend[...] = jnp.zeros((4, 8, 128), F32)
-    mst[...] = jnp.full((3, 2 * ROWS, 128), FLOOR, F32)
-    ast[...] = jnp.zeros((3, 2 * ROWS, 256), F32)
-
-    def out_copy(j, n):
-        to, where = peer_of(j)
+    lsend[...] = jnp.zeros((2, 8, 128), F32)
+    mst[...] = jnp.full((3, ROWS, 128), FLOOR, F32)
+    ast[...] = jnp.zeros((3, ROWS, 256), F32)
+
+    def out_copy(n):
         a, b = ((osend, orecv), (lsend, lrecv))[n]
-        return rcopy(a.at[to], b.at[w], os_.at[j, n], or_.at[j, n], where)
+        return rcopy(a.at[1 - z_lo], b.at[z_lo], os_.at[n], or_.at[n], partner)
 
     def ques_mask():
-        row = lax.broadcasted_iota(jnp.int32, (4 * QROWS, 1), 0)
-        row_pos = lax.div(row, 2 * QROWS) * 256 + g * 16 + lax.rem(row, 16)
+        row = lax.broadcasted_iota(jnp.int32, (2 * QROWS, 1), 0)
+        row_pos = lax.div(row, QROWS) * 256 + g * 16 + lax.rem(row, 16)
         col = lax.broadcasted_iota(jnp.int32, (1, 256), 1)
-        col_mine = lax.div(lax.rem(col, 16), 8) == b1
-        return jnp.where(col_mine, z_lo * 256 + col, 100000) <= row_pos
+        return z_lo * 256 + col <= row_pos
 
     def ques_pass(part):
         closing = (
@@ -527,13 +539,13 @@
             lambda: jnp.concatenate([kvq[1], ones[0:256]], axis=1), ques_mask,
         )
         attend(
-            1, 4 * QROWS, lambda b: jnp.concatenate([qall[j, ROWS:, :] for j in range(4)], axis=0),
+            1, 2 * QROWS, lambda b: jnp.concatenate([qall[j, ROWS:, :] for j in range(2)], axis=0),
             part, 4, closing, mst.at[2], ast.at[2],
         )
 
         @pl.when(part == NP - 1)
         def _():
-            for src in range(4):
+            for src in range(2):
                 rows = slice(src * QROWS, (src + 1) * QROWS)
                 total = ast[2, rows, 128:256]
                 osend[src, ROWS:, :] = (ast[2, rows, 0:128] / total).astype(BF16)
@@ -541,26 +553,24 @@
 
     def rec_pass(part, c):
         n_open = 2 * c + lax.div(g, 8)
-        pos_col = to_col(qpos[2 * c, 0:1, :], 128)
-        pos_col = jnp.concatenate([pos_col] * HEADS, axis=0)
+        pos_col = to_col(qpos[c, 0:1, :], 128)
+        pos_col = jnp.concatenate([pos_col] * 3, axis=0)
         key_pos = key_off + (n_open * (8 * PT) + part * TOK).astype(F32)
         closing = (
             None, lambda: kt[n_open], lambda: v_chunk(part, n_open),
             lambda: key_pos <= pos_col,
         )
         attend(
-            2, ROWS, lambda b: qall[2 * c + b, 0:ROWS, :],
+            2, 384, lambda b: qall[c, b * 384:(b + 1) * 384, :],
             part, n_open, closing, mst.at[c], ast.at[c],
         )
 
     def rec_end(c):
-        for b in range(2):
-            src = 2 * c + b
-            for hh in range(HEADS):
-                rows = slice(b * ROWS + hh * 128, b * ROWS + (hh + 1) * 128)
-                total = ast[c, rows, 128:256]
-                osend[src, hh * 128:(hh + 1) * 128, :] = (ast[c, rows, 0:128] / total).astype(BF16)
-                lsend[src, hh:hh + 1, :] = log_sum(mst[c, rows, :], total, 128)
+        for hh in range(HEADS):
+            rows = slice(hh * 128, (hh + 1) * 128)
+            total = ast[c, rows, 128:256]
+            osend[c, rows, :] = (ast[c, rows, 0:128] / total).astype(BF16)
+            lsend[c, hh:hh + 1, :] = log_sum(mst[c, rows, :], total, 128)
 
     @pl.loop(0, NP)
     def _(part):
@@ -571,11 +581,13 @@
         def _(t):
             @pl.when((part == 0) & (t == 0))
             def _():
-                g_first(1)
+                g_first(2)
+                g_first(3)
 
             @pl.when((part == 0) & (t == 1))
             def _():
-                g_second(1)
+                g_second(2)
+                g_second(3)
 
             c = lax.rem(z_lo + 1 + t, 2)
             rec_pass(part, c)
@@ -586,22 +598,17 @@
 
             @pl.when((part == NP - 1) & (t == 0))
             def _():
-                for j in range(2):
-                    for n in range(2):
-                        out_copy(j, n).start()
-
-            @pl.when((part == NP - 1) & (t == 1))
-            def _():
                 for n in range(2):
-                    out_copy(2, n).start()
+                    out_copy(n).start()
 
         @pl.when(part == 0)
         def _():
-            g_end(1)
-
-    orecv[w] = osend[w]
-    lrecv[w] = lsend[w]
-    out_copies = [out_copy(j, n) for j in range(3) for n in range(2)]
+            g_end(2)
+            g_end(3)
+
+    orecv[z_lo] = osend[z_lo]
+    lrecv[z_lo] = lsend[z_lo]
+    out_copies = [out_copy(n) for n in range(2)]
     for c in out_copies:
         c.wait_recv()
 
@@ -609,7 +616,7 @@
         cols_ = [to_col(l, n) for l in lses]
         top_ = functools.reduce(jnp.maximum, cols_)
         ws = [jnp.exp(c - top_) for c in cols_]
-        total = ws[0] + ws[1] + ws[2] + ws[3]
+        total = ws[0] + ws[1]
         acc = ws[0] * parts[0].astype(F32)
         for w, part in zip(ws[1:], parts[1:]):
             acc = acc + w * part.astype(F32)
@@ -620,17 +627,19 @@
     @pl.loop(0, HEADS)
     def _(hh):
         rows = pl.ds(pl.multiple_of(hh * 128, 128), 128)
-        o = join([orecv[j, rows, :] for j in range(4)], [lrecv[j, pl.ds(hh, 1), :] for j in range(4)], 128)
+        o = join([orecv[j, rows, :] for j in range(2)], [lrecv[j, pl.ds(hh, 1), :] for j in range(2)], 128)
         rec_out[:, rows] = jnp.where(used, o, 0.0).astype(BF16)
 
-    o = join([orecv[j, ROWS:, :] for j in range(4)], [lrecv[j, 6:7, :] for j in range(4)], QROWS)
+    o = join([orecv[j, ROWS:, :] for j in range(2)], [lrecv[j, 6:7, :] for j in range(2)], QROWS)
     for hh in range(HEADS):
         ques_out[:, hh * 128:(hh + 1) * 128] = o[hh * 16:(hh + 1) * 16].astype(BF16)
 
     for c in plain0 + plain1 + merged1 + z0 + z1 + q_copies + out_copies:
         c.wait_send()
-    for fam in range(3):
+    for fam in range(5):
         g_sent(fam)
+    for part in range(NP):
+        swap_copy(part).wait_send()
 
 
 def on_device(
@@ -664,25 +673,26 @@
             v((NP, 4, 2, TOK, 128), F32),
             v((NP, 4, TOK, 128), F32),
             v((NP, 4, 2, TOK, 256), F32),
-            v((NP, 2, 2, 16 * TOK, 128), BF16),
+            v((NP, 2, 2, 2, 16 * TOK, 128), BF16),
             v((2, 256, 128), BF16),
-            v((4, ROWS + QROWS, 128), BF16),
-            v((4, 8, 128), F32),
-            v((4, 128, CHUNK), BF16),
-            v((3, 2 * ROWS, 128), F32), v((3, 2 * ROWS, 256), F32),
-            v((4, ROWS + QROWS, 128), BF16),
-            v((4, ROWS + QROWS, 128), BF16),
-            v((4, 8, 128), F32),
-            v((4, 8, 128), F32),
+            v((2, ROWS + QROWS, 128), BF16),
+            v((2, 8, 128), F32),
+            v((4, 128, 2 * CHUNK), BF16),
+            v((3, ROWS, 128), F32), v((3, ROWS, 256), F32),
+            v((2, ROWS + QROWS, 128), BF16),
+            v((2, ROWS + QROWS, 128), BF16),
+            v((2, 8, 128), F32),
+            v((2, 8, 128), F32),
             dma((12,)),
             dma((NP, 2, 4)),
             dma((NP, 6, 2)), dma((NP, 6, 2)),
             dma((NP, 7)), dma((NP, 7)),
-            dma((3, 2)), dma((3, 2)),
-            dma((3, 4)), dma((3, 4)),
-            dma((3, 4)), dma((3, 4)),
-            dma((3, 8)), dma((3, 8)),
-            dma((3, 2)), dma((3, 2)),
+            dma((NP,)), dma((NP,)),
+            dma((2,)), dma((2,)),
+            dma((5, 4)), dma((5, 4)),
+            dma((5, 4)), dma((5, 4)),
+            dma((5, 8)), dma((5, 8)),
+            dma((2,)), dma((2,)),
         ],
         compiler_params=pltpu.CompilerParams(
             collective_id=0, has_side_effects=True, vmem_limit_bytes=VMEM_LIMIT

time: 107 us -> 96.6 us (0.903); the launches traced: 107 us -> 95 us
  Pallas kernels: 103 us -> 91.4 us
    pallas_call x1, Pallas kernels: 103 us -> 91.4 us  [on_device(): pl.pallas_call(kernel, out_shape=(jax.ShapeDtypeStruct((RECP, HEADS * HD)...]
where the time goes in v4:
time: 96.6 us; the launch traced here: 95 us
  Pallas kernels  91.4 us (95%)
  local copies, waits for them, and re-layouts  2.23 us (2%)
  between operations  1.3 us (1%)
    pallas_call x1, Pallas kernels, on_device(): pl.pallas_call(kernel, out_shape=(jax.ShapeDtypeStruct((RECP, HEADS * HD)...  91.4 us
    unnamed x4, local copies, waits for them, and re-layouts  2.23 us

profile of v4, /device:TPU:56, one launch (start us, length us, event | category | flops | bytes accessed | tf_op | source)
XLA Modules:
  0.0 95.0 jit_solution(2908390658628888190)
XLA Ops:
  1.3 91.4 %blend_attend.1 = (bf16[128,768]{1,0:T(8,128)(2,1)}, bf16[16,768]{1,0:T(8,128)(2,1)}) custom-call(s32[512]{0:T(512)} %pos_off_h.1, s32[512]{0:T(512)} %owner_map_h.1, s32[32]{0:T(128)} %pids_h.1, s32[1]{0:T(128)S(6)} %copy.18.rec_count_h, s32[1,128]{1,0:T(1,128)} %rec_index_h.1, f32[1,128]{1,0:T(1,128)} %constant.2.clone.freq_h, bf16[128,768]{1,0:T(8,128)(2,1)} %fresh_q_h.1, ...), custom_call_target="tpu_custom_call" | custom-call | flops 8000000000 | bytes 4000000 | tf_op jit(solution)/shard_map/blend_attend/pallas_call | solution.py:655
  92.7 0.0 copy-start
  92.7 1.6 %copy.19 = bf16[128,768]{1,0:T(8,128)(2,1)} copy(bf16[128,768]{1,0:T(8,128)(2,1)} %get-tuple-element.4) | data formatting | bytes 393216
  94.4 0.0 copy-done
  94.4 0.6 copy.20
Async XLA Ops:
  92.7 1.6 %copy-start = (bf16[16,768]{1,0:T(8,128)(2,1)S(1)}, bf16[16,768]{1,0:T(8,128)(2,1)}, u32[]{:S(2)}) copy-start(bf16[16,768]{1,0:T(8,128)(2,1)} %get-tuple-element.5) | copy-start | bytes 73732

commit v5 on v4

--- a/solution.py
+++ b/solution.py
@@ -18,8 +18,8 @@
 QROWS = HEADS * QDEV
 QSTART = PASS * PT
 CHUNK = 512
-NP = 2
-TOK = 64
+NP = 4
+TOK = 32
 VMEM_LIMIT = 62 * 1024 * 1024
 FLOOR = -1e30
 SCALE = float(1.0 / np.sqrt(128.0))
@@ -85,14 +85,11 @@
     fresh_v_h, ques_q_h, ques_k_h, ques_v_h, k_store, v_store,
     rec_out, ques_out,
     pos_off, owner_map, pids, rec_count, rec_index, freq_ref, fresh_q, fresh_kv, ques_q, ques_kv,
-    xfin0, xfin1, mb00, mb01, mb10, mb11, msend, zsend, zin0, zin1, tab, keep, repl, kvall, kvq,
+    xfin, mbuf, msend, zsend, zin, tab, keep, repl, kvall, kvq,
     qall, qpos, kt, mst, ast,
     osend, orecv, lsend, lrecv,
     isem, lsem, xs, xr, zs, zr, bs, br, qs, qr, ps, pr, ns, nr, cs, cr, os_, or_,
 ):
-    xfin = (xfin0, xfin1)
-    mbuf = ((mb00, mb01), (mb10, mb11))
-    zin = (zin0, zin1)
     bank = lax.axis_index("bank")
     blk = lax.axis_index("blk")
     x = lax.div(bank, 4)
@@ -218,7 +215,8 @@
             copies.append(c)
         return copies
 
-    def x_finish(part, plain, merged, owner_x, between):
+    def x_finish(part, plain, merged, owner_x):
+        at_tok = slice(part * TOK, (part + 1) * TOK)
         for kv in range(2):
             loc[part][kv * 4 + 2].wait()
             loc[part][kv * 4 + 3].wait()
@@ -236,13 +234,11 @@
                     lanes = slice(hh * 128, (hh + 1) * 128)
                     piece = data[:, lanes]
                     if kv == 0:
-                        piece = turn(piece, tab[part, quarter, 0], tab[part, quarter, 1])
+                        piece = turn(piece, tab[quarter, 0, at_tok], tab[quarter, 1, at_tok])
                     else:
-                        piece = piece * keep[part, quarter]
-                    piece = piece + repl[part, quarter, kv, :, lanes]
+                        piece = piece * keep[quarter, at_tok]
+                    piece = piece + repl[quarter, kv, at_tok, lanes]
                     zsend[part, hh, quarter, kv] = piece.astype(BF16)
-            if kv == 0 and between is not None:
-                between()
         copies = []
         for i in (1, 7, 2, 6, 3, 5, 4):
             t = lax.rem(zc + i, 8)
@@ -271,87 +267,89 @@
             kvall[part, b1, 0, c, g_rows(g), :] = zin[part][idx, 0]
             kvall[part, b1, 1, c, g_rows(g), :] = zin[part][idx, 1]
         swap_copy(part).start()
-        g_start(2 * part)
+        g_start(part, 0)
 
     def swap_finish(part):
         piece = kvall.at[part, 1 - b1, :, :, g_rows(g), :]
         rcopy(piece, piece, bs.at[part], br.at[part], other_b).wait_recv()
-        g_start(2 * part + 1)
-
-    def gather_slices(fam, gg):
-        if fam < 4:
-            return kvall.at[fam // 2, b1 if fam % 2 == 0 else 1 - b1, :, :, g_rows(gg), :]
+        g_start(part, 1)
+
+    def gather_slices(part, o, gg):
+        if o < 2:
+            return kvall.at[part, b1 if o == 0 else 1 - b1, :, :, g_rows(gg), :]
         return kvq.at[:, pl.ds(pl.multiple_of(gg * 16, 16), 16), :]
 
-    def reach(fam):
-        return (4, 3) if fam % 2 == 0 else (3, 4)
+    def reach(o):
+        return (4, 3) if o % 2 == 0 else (3, 4)
 
     def at_y(dy):
         return lax.rem(y + 8 + dy, 8) * 2 + core
 
-    def g_copy(fam, dy, which, hop):
-        piece = gather_slices(fam, at_y(dy))
+    def g_copy(part, o, dy, which, hop):
+        piece = gather_slices(part, o, at_y(dy))
+        fam = 2 * NP if o == 2 else 2 * part + o
         if which == "up":
             return rcopy(piece, piece, ps.at[fam, hop], pr.at[fam, hop], y_up2 if hop % 2 else y_up)
         if which == "dn":
             return rcopy(piece, piece, ns.at[fam, hop], nr.at[fam, hop], y_dn2 if hop % 2 else y_dn)
         return rcopy(piece, piece, cs.at[fam, hop], cr.at[fam, hop], twin)
 
-    def g_send(fam, dy, which, hop):
-        g_copy(fam, dy, which, hop).start()
-
-    def g_arrived(fam, dy, which, hop):
-        g_copy(fam, dy, which, hop).wait_recv()
-
-    def g_start(fam):
-        for hop in range(2):
-            g_send(fam, 0, "up", hop)
-            g_send(fam, 0, "dn", hop)
-        g_send(fam, 0, "twin", 0)
-
-    def g_first(fam):
-        n_up, n_dn = reach(fam)
-        g_arrived(fam, -2, "up", 1)
+    def g_send(part, o, dy, which, hop):
+        g_copy(part, o, dy, which, hop).start()
+
+    def g_arrived(part, o, dy, which, hop):
+        g_copy(part, o, dy, which, hop).wait_recv()
+
+    def g_start(part, o):
+        for hop in (1, 0):
+            g_send(part, o, 0, "up", hop)
+            g_send(part, o, 0, "dn", hop)
+        g_send(part, o, 0, "twin", 0)
+
+    def g_first(part, o):
+        n_up, n_dn = reach(o)
+        g_arrived(part, o, -2, "up", 1)
         for hop in range(2, n_up):
-            g_send(fam, -2, "up", hop)
-        g_arrived(fam, 2, "dn", 1)
+            g_send(part, o, -2, "up", hop)
+        g_arrived(part, o, 2, "dn", 1)
         for hop in range(2, n_dn):
-            g_send(fam, 2, "dn", hop)
-        g_send(fam, -2, "twin", 2)
-        g_send(fam, 2, "twin", 6)
-        g_arrived(fam, -1, "up", 0)
-        g_send(fam, -1, "twin", 1)
-        g_arrived(fam, 1, "dn", 0)
-        g_send(fam, 1, "twin", 5)
-
-    def g_second(fam):
-        n_up, n_dn = reach(fam)
+            g_send(part, o, 2, "dn", hop)
+        g_send(part, o, -2, "twin", 2)
+        g_send(part, o, 2, "twin", 6)
+        g_arrived(part, o, -1, "up", 0)
+        g_send(part, o, -1, "twin", 1)
+        g_arrived(part, o, 1, "dn", 0)
+        g_send(part, o, 1, "twin", 5)
+
+    def g_second(part, o):
+        n_up, n_dn = reach(o)
         for d in range(3, n_up + 1):
-            g_arrived(fam, -d, "up", d - 1)
-            g_send(fam, -d, "twin", d)
+            g_arrived(part, o, -d, "up", d - 1)
+            g_send(part, o, -d, "twin", d)
         for d in range(3, n_dn + 1):
-            g_arrived(fam, d, "dn", d - 1)
-            g_send(fam, d, "twin", d if d == 4 else 4 + d)
-
-    def twin_hops(fam):
-        n_up, n_dn = reach(fam)
+            g_arrived(part, o, d, "dn", d - 1)
+            g_send(part, o, d, "twin", d if d == 4 else 4 + d)
+
+    def twin_hops(o):
+        n_up, n_dn = reach(o)
         return [(0, 0)] + [(-d, d) for d in range(1, n_up + 1)] + [
             (d, d if d == 4 else 4 + d) for d in range(1, n_dn + 1)
         ]
 
-    def g_end(fam):
-        for dy, hop in twin_hops(fam):
-            piece = gather_slices(fam, lax.rem(y + 8 + dy, 8) * 2 + 1 - core)
+    def g_end(part, o):
+        fam = 2 * NP if o == 2 else 2 * part + o
+        for dy, hop in twin_hops(o):
+            piece = gather_slices(part, o, lax.rem(y + 8 + dy, 8) * 2 + 1 - core)
             rcopy(piece, piece, cs.at[fam, hop], cr.at[fam, hop], twin).wait_recv()
 
-    def g_sent(fam):
-        n_up, n_dn = reach(fam)
+    def g_sent(part, o):
+        n_up, n_dn = reach(o)
         for hop in range(n_up):
-            g_copy(fam, 0 if hop < 2 else -2, "up", hop).wait_send()
+            g_copy(part, o, 0 if hop < 2 else -2, "up", hop).wait_send()
         for hop in range(n_dn):
-            g_copy(fam, 0 if hop < 2 else 2, "dn", hop).wait_send()
-        for dy, hop in twin_hops(fam):
-            g_copy(fam, dy, "twin", hop).wait_send()
+            g_copy(part, o, 0 if hop < 2 else 2, "dn", hop).wait_send()
+        for dy, hop in twin_hops(o):
+            g_copy(part, o, dy, "twin", hop).wait_send()
 
     relay0 = x_relay(0)
     for c in moves:
@@ -363,6 +361,40 @@
 
     freq = freq_ref[...]
     rec_row = rec_index[...].astype(F32)
+    off_f = off.astype(F32)
+    base_f = (blk * PT).astype(F32)
+    slot_lane = lax.broadcasted_iota(jnp.int32, (128, 128), 1)
+
+    @pl.loop(0, 4)
+    def _(quarter):
+        first = quarter * 128
+        tok = lax.broadcasted_iota(jnp.int32, (128, 128), 0) + first
+        match = (tok.astype(F32) == jnp.broadcast_to(rec_row, (128, 128))) & (slot_lane < count)
+        onehot = jnp.where(match, 1.0, 0.0)
+        found = jnp.sum(onehot, axis=1, keepdims=True) > 0.5
+        onehot = onehot.astype(BF16)
+        tpos = (lax.broadcasted_iota(jnp.int32, (128, 1), 0) + first).astype(F32) + base_f
+        tpos = tpos - jnp.where(found, 0.0, off_f)
+        c_t, s_t = cos_sin(tpos, freq)
+        rk = jnp.dot(onehot, fresh_kv[0], preferred_element_type=F32)
+        for hh in range(2):
+            lanes = slice(hh * 128, (hh + 1) * 128)
+            repl[quarter, 0, :, lanes] = turn(rk[:, lanes], c_t, s_t)
+        repl[quarter, 1] = jnp.dot(onehot, fresh_kv[1], preferred_element_type=F32)
+        stay = jnp.broadcast_to(jnp.where(found, 0.0, 1.0), (128, 128))
+        keep[quarter] = stay
+        tab[quarter, 0] = c_t * stay
+        tab[quarter, 1] = s_t * stay
+
+
+    def after(copies):
+        for c in copies:
+            c.wait_send()
+
+    after(relay0)
+    plain0 = x_plain(0)
+    merged0 = x_merge(0, relay0, owner_x)
+
     rec_pos_row = rec_row + (blk * PT).astype(F32)
     rec_pos = to_col(rec_pos_row, 128)
     c_rec, s_rec = cos_sin(rec_pos, freq)
@@ -374,9 +406,6 @@
         qall[z_lo, at, :] = q.astype(BF16)
 
     qpos[z_lo] = jnp.broadcast_to(rec_pos_row, (8, 128))
-    for c in relay0:
-        c.wait_send()
-    plain0 = x_plain(0)
     ques_pos = (
         lax.broadcasted_iota(jnp.int32, (QDEV, 1), 0) + (QSTART + blk * QDEV)
     ).astype(F32)
@@ -394,64 +423,51 @@
     my_rows = pl.ds(pl.multiple_of(g * 16, 16), 16)
     kvq[0, my_rows, :] = turn(ques_kv[0].astype(F32), c_q, s_q).astype(BF16)
     kvq[1, my_rows, :] = ques_kv[1]
-    merged0 = x_merge(0, relay0, owner_x)
-    g_start(4)
-
-    off_f = off.astype(F32)
-    base_f = (blk * PT).astype(F32)
-    slot_lane = lax.broadcasted_iota(jnp.int32, (TOK, 128), 1)
-
-    def tables(part):
-        @pl.loop(0, 4)
-        def _(quarter):
-            first = quarter * 128 + part * TOK
-            tok = lax.broadcasted_iota(jnp.int32, (TOK, 128), 0) + first
-            match = (tok.astype(F32) == jnp.broadcast_to(rec_row, (TOK, 128))) & (slot_lane < count)
-            onehot = jnp.where(match, 1.0, 0.0)
-            found = jnp.sum(onehot, axis=1, keepdims=True) > 0.5
-            onehot = onehot.astype(BF16)
-            tpos = (lax.broadcasted_iota(jnp.int32, (TOK, 1), 0) + first).astype(F32) + base_f
-            tpos = tpos - jnp.where(found, 0.0, off_f)
-            c_t, s_t = cos_sin(tpos, freq)
-            rk = jnp.dot(onehot, fresh_kv[0], preferred_element_type=F32)
-            for hh in range(2):
-                lanes = slice(hh * 128, (hh + 1) * 128)
-                repl[part, quarter, 0, :, lanes] = turn(rk[:, lanes], c_t, s_t)
-            repl[part, quarter, 1] = jnp.dot(onehot, fresh_kv[1], preferred_element_type=F32)
-            stay = jnp.broadcast_to(jnp.where(found, 0.0, 1.0), (TOK, 128))
-            keep[part, quarter] = stay
-            tab[part, quarter, 0] = c_t * stay
-            tab[part, quarter, 1] = s_t * stay
-
-    tables(0)
-    for c in merged0:
-        c.wait_send()
+    g_start(0, 2)
+    after(merged0)
     relay1 = x_relay(1)
-    tables(1)
-    plain1 = []
-
-    def go_plain1():
-        for c in relay1:
-            c.wait_send()
-        plain1.extend(x_plain(1))
-
-    z0 = x_finish(0, plain0, merged0, owner_x, go_plain1)
+    z0 = x_finish(0, plain0, merged0, owner_x)
+    after(relay1)
+    plain1 = x_plain(1)
     merged1 = x_merge(1, relay1, owner_x)
-    g_first(4)
-    g_second(4)
+    after(merged1)
+    relay2 = x_relay(2)
+    z1 = x_finish(1, plain1, merged1, owner_x)
+    after(relay2)
+    plain2 = x_plain(2)
+    merged2 = x_merge(2, relay2, owner_x)
+    g_first(0, 2)
     z_finish(0, z0)
+    after(merged2)
+    relay3 = x_relay(3)
+    z2 = x_finish(2, plain2, merged2, owner_x)
+    after(relay3)
+    plain3 = x_plain(3)
+    merged3 = x_merge(3, relay3, owner_x)
     swap_finish(0)
-    z1 = x_finish(1, plain1, merged1, owner_x, None)
-    for step in (g_first, g_second):
-        step(0)
-        step(1)
     z_finish(1, z1)
-    g_end(4)
-    g_end(0)
-    g_end(1)
+    g_first(0, 0)
+    g_second(0, 2)
+    z3 = x_finish(3, plain3, merged3, owner_x)
+    g_first(0, 1)
+    swap_finish(1)
+    g_first(1, 0)
+    z_finish(2, z2)
+    g_second(0, 0)
+    g_second(0, 1)
+    g_first(1, 1)
+    swap_finish(2)
+    g_first(2, 0)
+    z_finish(3, z3)
+    g_second(1, 0)
+    g_second(1, 1)
+    g_first(2, 1)
+    swap_finish(3)
+    g_end(0, 2)
+    g_end(0, 0)
+    g_end(0, 1)
     for c in q_copies:
         c.wait_recv()
-    swap_finish(1)
 
     key_lane = lax.broadcasted_iota(jnp.int32, (1, 2 * CHUNK), 1)
     key_in = lax.rem(key_lane, CHUNK)
@@ -460,12 +476,10 @@
     ones = jnp.ones((2 * CHUNK, 128), BF16)
 
     def chunk_of(part, b, kv, ch):
-        rows = pl.ds(pl.multiple_of(lax.rem(ch, 2) * CHUNK, CHUNK), CHUNK)
-        return kvall[part, b, kv, lax.div(ch, 2), rows, :]
+        return kvall[part, b, kv, ch]
 
     def transpose_keys(part):
-        @pl.loop(0, 4)
-        def _(ch):
+        for ch in range(2):
             for b in range(2):
                 kt[ch, :, b * CHUNK:(b + 1) * CHUNK] = jnp.transpose(chunk_of(part, b, 0, ch))
 
@@ -540,7 +554,7 @@
         )
         attend(
             1, 2 * QROWS, lambda b: jnp.concatenate([qall[j, ROWS:, :] for j in range(2)], axis=0),
-            part, 4, closing, mst.at[2], ast.at[2],
+            part, 2, closing, mst.at[2], ast.at[2],
         )
 
         @pl.when(part == NP - 1)
@@ -552,10 +566,10 @@
                 lsend[src, 6:7, :] = log_sum(mst[2, rows, :], total, QROWS)
 
     def rec_pass(part, c):
-        n_open = 2 * c + lax.div(g, 8)
+        n_open = c
         pos_col = to_col(qpos[c, 0:1, :], 128)
         pos_col = jnp.concatenate([pos_col] * 3, axis=0)
-        key_pos = key_off + (n_open * (8 * PT) + part * TOK).astype(F32)
+        key_pos = key_off + (n_open * (16 * PT) + part * TOK).astype(F32)
         closing = (
             None, lambda: kt[n_open], lambda: v_chunk(part, n_open),
             lambda: key_pos <= pos_col,
@@ -581,13 +595,15 @@
         def _(t):
             @pl.when((part == 0) & (t == 0))
             def _():
-                g_first(2)
-                g_first(3)
-
-            @pl.when((part == 0) & (t == 1))
+                g_first(3, 0)
+                g_second(2, 0)
+                g_second(2, 1)
+                g_first(3, 1)
+
+            @pl.when((part == 1) & (t == 0))
             def _():
-                g_second(2)
-                g_second(3)
+                g_second(3, 0)
+                g_second(3, 1)
 
             c = lax.rem(z_lo + 1 + t, 2)
             rec_pass(part, c)
@@ -601,10 +617,10 @@
                 for n in range(2):
                     out_copy(n).start()
 
-        @pl.when(part == 0)
+        @pl.when(part < NP - 1)
         def _():
-            g_end(2)
-            g_end(3)
+            g_end(part + 1, 0)
+            g_end(part + 1, 1)
 
     orecv[z_lo] = osend[z_lo]
     lrecv[z_lo] = lsend[z_lo]
@@ -634,11 +650,14 @@
     for hh in range(HEADS):
         ques_out[:, hh * 128:(hh + 1) * 128] = o[hh * 16:(hh + 1) * 16].astype(BF16)
 
-    for c in plain0 + plain1 + merged1 + z0 + z1 + q_copies + out_copies:
+    for c in plain0 + plain1 + plain2 + plain3 + merged3 + z0 + z1 + z2 + z3 + q_copies + out_copies:
         c.wait_send()
-    for fam in range(5):
-        g_sent(fam)
-    for part in range(NP):
+    g_sent(0, 2)
+
+    @pl.loop(0, NP)
+    def _(part):
+        g_sent(part, 0)
+        g_sent(part, 1)
         swap_copy(part).wait_send()
 
 
@@ -664,20 +683,19 @@
             smem((512,), i32), smem((512,), i32), smem((32,), i32), smem((1,), i32),
             v((1, 128), i32), v((1, 128), F32), v((RECP, HEADS * HD), BF16),
             v((2, RECP, 256), BF16), v((QDEV, HEADS * HD), BF16), v((2, QDEV, 128), BF16),
-            v((3, 2, 2, 2, TOK, 256), BF16), v((3, 2, 2, 2, TOK, 256), BF16),
-            v((2, 2, 2, TOK, 256), BF16), v((2, 2, 2, TOK, 256), BF16),
-            v((2, 2, 2, TOK, 256), BF16), v((2, 2, 2, TOK, 256), BF16),
+            (v((3, 2, 2, 2, TOK, 256), BF16),) * NP,
+            ((v((2, 2, 2, TOK, 256), BF16),) * 2,) * NP,
             v((NP, 2, 2, 2, TOK, 256), BF16),
             v((NP, 2, 4, 2, TOK, 128), BF16),
-            v((8, 2, TOK, 128), BF16), v((8, 2, TOK, 128), BF16),
-            v((NP, 4, 2, TOK, 128), F32),
-            v((NP, 4, TOK, 128), F32),
-            v((NP, 4, 2, TOK, 256), F32),
+            (v((8, 2, TOK, 128), BF16),) * NP,
+            v((4, 2, 128, 128), F32),
+            v((4, 128, 128), F32),
+            v((4, 2, 128, 256), F32),
             v((NP, 2, 2, 2, 16 * TOK, 128), BF16),
             v((2, 256, 128), BF16),
             v((2, ROWS + QROWS, 128), BF16),
             v((2, 8, 128), F32),
-            v((4, 128, 2 * CHUNK), BF16),
+            v((2, 128, 2 * CHUNK), BF16),
             v((3, ROWS, 128), F32), v((3, ROWS, 256), F32),
             v((2, ROWS + QROWS, 128), BF16),
             v((2, ROWS + QROWS, 128), BF16),
@@ -689,9 +707,9 @@
             dma((NP, 7)), dma((NP, 7)),
             dma((NP,)), dma((NP,)),
             dma((2,)), dma((2,)),
-            dma((5, 4)), dma((5, 4)),
-            dma((5, 4)), dma((5, 4)),
-            dma((5, 8)), dma((5, 8)),
+            dma((9, 4)), dma((9, 4)),
+            dma((9, 4)), dma((9, 4)),
+            dma((9, 8)), dma((9, 8)),
             dma((2,)), dma((2,)),
         ],
         compiler_params=pltpu.CompilerParams(

time: 96.6 us -> 99.6 us (1.031)
  Pallas kernels: 91.4 us -> 94.4 us
    pallas_call x1, Pallas kernels: 91.4 us -> 94.4 us  [on_device(): pl.pallas_call(kernel, out_shape=(jax.ShapeDtypeStruct((RECP, HEADS * HD)...]
where the time goes in v5:
time: 99.6 us; the launch traced here: 97.9 us
  Pallas kernels  94.4 us (95%)
  local copies, waits for them, and re-layouts  2.23 us (2%)
  between operations  1.3 us (1%)
    pallas_call x1, Pallas kernels, on_device(): pl.pallas_call(kernel, out_shape=(jax.ShapeDtypeStruct((RECP, HEADS * HD)...  94.4 us
    unnamed x4, local copies, waits for them, and re-layouts  2.23 us

profile of v5, /device:TPU:56, one launch (start us, length us, event | category | flops | bytes accessed | tf_op | source)
XLA Modules:
  0.0 97.9 jit_solution(13370791528464686717)
XLA Ops:
  1.3 94.4 %blend_attend.1 = (bf16[128,768]{1,0:T(8,128)(2,1)}, bf16[16,768]{1,0:T(8,128)(2,1)}) custom-call(s32[512]{0:T(512)} %pos_off_h.1, s32[512]{0:T(512)} %owner_map_h.1, s32[32]{0:T(128)} %pids_h.1, s32[1]{0:T(128)S(6)} %copy.18.rec_count_h, s32[1,128]{1,0:T(1,128)} %rec_index_h.1, f32[1,128]{1,0:T(1,128)} %constant.2.clone.freq_h, bf16[128,768]{1,0:T(8,128)(2,1)} %fresh_q_h.1, ...), custom_call_target="tpu_custom_call" | custom-call | flops 8000000000 | bytes 4000000 | tf_op jit(solution)/shard_map/blend_attend/pallas_call | solution.py:674
  95.7 0.0 copy-start
  95.7 1.6 %copy.19 = bf16[128,768]{1,0:T(8,128)(2,1)} copy(bf16[128,768]{1,0:T(8,128)(2,1)} %get-tuple-element.4) | data formatting | bytes 393216
  97.3 0.0 copy-done
  97.3 0.6 copy.20
Async XLA Ops:
  95.7 1.6 %copy-start = (bf16[16,768]{1,0:T(8,128)(2,1)S(1)}, bf16[16,768]{1,0:T(8,128)(2,1)}, u32[]{:S(2)}) copy-start(bf16[16,768]{1,0:T(8,128)(2,1)} %get-tuple-element.5) | copy-start | bytes 73732

commit v6 on v4

--- a/solution.py
+++ b/solution.py
@@ -85,13 +85,11 @@
     fresh_v_h, ques_q_h, ques_k_h, ques_v_h, k_store, v_store,
     rec_out, ques_out,
     pos_off, owner_map, pids, rec_count, rec_index, freq_ref, fresh_q, fresh_kv, ques_q, ques_kv,
-    xfin0, xfin1, mb00, mb01, mb10, mb11, msend, zsend, zin0, zin1, tab, keep, repl, kvall, kvq,
+    stage, xfin, mbuf, msend, zsend, zin0, zin1, tab, keep, repl, kvall,
     qall, qpos, kt, mst, ast,
     osend, orecv, lsend, lrecv,
     isem, lsem, xs, xr, zs, zr, bs, br, qs, qr, ps, pr, ns, nr, cs, cr, os_, or_,
 ):
-    xfin = (xfin0, xfin1)
-    mbuf = ((mb00, mb01), (mb10, mb11))
     zin = (zin0, zin1)
     bank = lax.axis_index("bank")
     blk = lax.axis_index("blk")
@@ -150,55 +148,38 @@
     for c in moves:
         c.start()
 
-    stores = (k_store, v_store)
+    staged = []
+    for kv, st in enumerate((k_store, v_store)):
+        for t in range(4):
+            c = pltpu.make_async_copy(st.at[:, :, t * 256:(t + 1) * 256], stage.at[t, kv], lsem.at[kv, t])
+            c.start()
+            staged.append(c)
     top = pl.ds(0, 2)
     low = pl.ds(2, 2)
 
     def toks(part):
         return pl.ds(part * TOK, TOK)
 
-    def x_local(part):
-        copies = []
-        for kv in range(2):
-            st = stores[kv]
-            for j, (src, dst) in enumerate((
-                (st.at[top, toks(part), cols(x + 1)], mbuf[part][0].at[0, kv]),
-                (st.at[low, toks(part), cols(x + 3)], mbuf[part][1].at[0, kv]),
-                (st.at[top, toks(part), cols(x)], xfin[part].at[0, kv, 0]),
-                (st.at[low, toks(part), cols(x)], xfin[part].at[0, kv, 1]),
-            )):
-                c = pltpu.make_async_copy(src, dst, lsem.at[part, kv, j])
-                c.start()
-                copies.append(c)
-        return copies
-
-    loc = [x_local(part) for part in range(NP)]
+    for c in staged:
+        c.wait()
     pl.semaphore_wait(barrier, len(peers))
 
     def x_relay(part):
-        copies = []
-        for kv in range(2):
-            st = stores[kv]
-            copies += [
-                rcopy(st.at[top, toks(part), cols(x + 2)], mbuf[part][0].at[1, kv],
-                      xs.at[part, 0, kv], xr.at[part, 0, kv], x_up),
-                rcopy(st.at[low, toks(part), cols(x + 2)], mbuf[part][1].at[1, kv],
-                      xs.at[part, 1, kv], xr.at[part, 1, kv], x_dn),
-            ]
+        far = lax.rem(x + 2, 4)
+        copies = [
+            rcopy(stage.at[far, :, top, toks(part)], mbuf.at[part, 0], xs.at[part, 0], xr.at[part, 0], x_up),
+            rcopy(stage.at[far, :, low, toks(part)], mbuf.at[part, 1], xs.at[part, 1], xr.at[part, 1], x_dn),
+        ]
         for c in copies:
             c.start()
         return copies
 
     def x_plain(part):
-        copies = []
-        for kv in range(2):
-            st = stores[kv]
-            copies += [
-                rcopy(st.at[low, toks(part), cols(x + 1)], xfin[part].at[1, kv, 1],
-                      xs.at[part, 2, kv], xr.at[part, 2, kv], x_up),
-                rcopy(st.at[top, toks(part), cols(x + 3)], xfin[part].at[2, kv, 0],
-                      xs.at[part, 3, kv], xr.at[part, 3, kv], x_dn),
-            ]
+        up, dn = lax.rem(x + 1, 4), lax.rem(x + 3, 4)
+        copies = [
+            rcopy(stage.at[up, :, low, toks(part)], xfin.at[part, 0, :, low], xs.at[part, 2], xr.at[part, 2], x_up),
+            rcopy(stage.at[dn, :, top, toks(part)], xfin.at[part, 1, :, top], xs.at[part, 3], xr.at[part, 3], x_dn),
+        ]
         for c in copies:
             c.start()
         return copies
@@ -206,32 +187,32 @@
     def x_merge(part, relay, owner_x):
         copies = []
         for d in range(2):
-            for kv in range(2):
-                loc[part][kv * 4 + d].wait()
-                relay[kv * 2 + d].wait_recv()
-            near = lax.rem(x + (3 if d == 0 else 1), 4)
-            pick = jnp.where(owner_x == near, 1, 0)
-            msend[part, d] = mbuf[part][d][pick]
-            c = rcopy(msend.at[part, d], xfin[part].at[1 + d, :, d],
-                      xs.at[part, 4 + d, 0], xr.at[part, 4 + d, 0], x_up if d == 0 else x_dn)
+            half = (top, low)[d]
+            relay[d].wait_recv()
+            target = lax.rem(x + (1 if d == 0 else 3), 4)
+            source = lax.rem(x + (3 if d == 0 else 1), 4)
+            mine = stage[target, :, half, toks(part), :]
+            msend[part, d] = jnp.where(owner_x == source, mbuf[part, d], mine)
+            c = rcopy(msend.at[part, d], xfin.at[part, d, :, half], xs.at[part, 4 + d], xr.at[part, 4 + d],
+                      x_up if d == 0 else x_dn)
             c.start()
             copies.append(c)
         return copies
 
     def x_finish(part, plain, merged, owner_x, between):
-        for kv in range(2):
-            loc[part][kv * 4 + 2].wait()
-            loc[part][kv * 4 + 3].wait()
         for c in plain + merged:
             c.wait_recv()
         is_own = owner_x == x
-        idx_a = jnp.where(is_own, 0, jnp.where(owner_x == lax.rem(x + 1, 4), 2, 1))
-        idx_b = jnp.where(is_own, 0, jnp.where(owner_x == lax.rem(x + 3, 4), 1, 2))
+        from_up = owner_x == lax.rem(x + 1, 4)
+        from_dn = owner_x == lax.rem(x + 3, 4)
         for kv in range(2):
             for quarter in range(4):
-                half = quarter // 2
-                idx = idx_a if half == 0 else idx_b
-                data = xfin[part][idx, kv, half, quarter % 2].astype(F32)
+                sides = [xfin[part, side, kv, quarter] for side in range(2)]
+                if quarter < 2:
+                    data = jnp.where(from_up, sides[1], sides[0])
+                else:
+                    data = jnp.where(from_dn, sides[0], sides[1])
+                data = jnp.where(is_own, stage[x, kv, quarter, toks(part), :], data).astype(F32)
                 for hh in range(2):
                     lanes = slice(hh * 128, (hh + 1) * 128)
                     piece = data[:, lanes]
@@ -255,11 +236,11 @@
         zin[part][0] = zsend[part, zh, z4]
         return copies
 
-    def g_rows(gg):
-        return pl.ds(pl.multiple_of(gg * TOK, TOK), TOK)
+    def rows_of(b, kv, c):
+        return pl.ds(pl.multiple_of(((b * 2 + kv) * 2 + c) * TOK, TOK), TOK)
 
     def swap_copy(part):
-        piece = kvall.at[part, b1, :, :, g_rows(g), :]
+        piece = kvall.at[part, g, pl.ds(pl.multiple_of(b1 * 4 * TOK, 4 * TOK), 4 * TOK), :]
         return rcopy(piece, piece, bs.at[part], br.at[part], other_b)
 
     def z_finish(part, copies):
@@ -268,20 +249,17 @@
         for c in range(2):
             owner_z = lax.rem(lax.div(owner_map[pids[c * 16 + g]], 32), 4)
             idx = lax.rem(zc + 8 - (2 * owner_z + c), 8)
-            kvall[part, b1, 0, c, g_rows(g), :] = zin[part][idx, 0]
-            kvall[part, b1, 1, c, g_rows(g), :] = zin[part][idx, 1]
+            for kv in range(2):
+                kvall[part, g, rows_of(b1, kv, c), :] = zin[part][idx, kv]
         swap_copy(part).start()
-        g_start(2 * part)
 
     def swap_finish(part):
-        piece = kvall.at[part, 1 - b1, :, :, g_rows(g), :]
+        piece = kvall.at[part, g, pl.ds(pl.multiple_of((1 - b1) * 4 * TOK, 4 * TOK), 4 * TOK), :]
         rcopy(piece, piece, bs.at[part], br.at[part], other_b).wait_recv()
-        g_start(2 * part + 1)
+        g_start(part)
 
     def gather_slices(fam, gg):
-        if fam < 4:
-            return kvall.at[fam // 2, b1 if fam % 2 == 0 else 1 - b1, :, :, g_rows(gg), :]
-        return kvq.at[:, pl.ds(pl.multiple_of(gg * 16, 16), 16), :]
+        return kvall.at[fam, gg, pl.ds(0, 8 * TOK + (32 if fam == 0 else 0)), :]
 
     def reach(fam):
         return (4, 3) if fam % 2 == 0 else (3, 4)
@@ -391,11 +369,9 @@
         c.start()
         q_copies.append(c)
 
-    my_rows = pl.ds(pl.multiple_of(g * 16, 16), 16)
-    kvq[0, my_rows, :] = turn(ques_kv[0].astype(F32), c_q, s_q).astype(BF16)
-    kvq[1, my_rows, :] = ques_kv[1]
+    kvall[0, g, 8 * TOK:8 * TOK + 16, :] = turn(ques_kv[0].astype(F32), c_q, s_q).astype(BF16)
+    kvall[0, g, 8 * TOK + 16:8 * TOK + 32, :] = ques_kv[1]
     merged0 = x_merge(0, relay0, owner_x)
-    g_start(4)
 
     off_f = off.astype(F32)
     base_f = (blk * PT).astype(F32)
@@ -437,21 +413,16 @@
 
     z0 = x_finish(0, plain0, merged0, owner_x, go_plain1)
     merged1 = x_merge(1, relay1, owner_x)
-    g_first(4)
-    g_second(4)
     z_finish(0, z0)
+    z1 = x_finish(1, plain1, merged1, owner_x, None)
     swap_finish(0)
-    z1 = x_finish(1, plain1, merged1, owner_x, None)
-    for step in (g_first, g_second):
-        step(0)
-        step(1)
     z_finish(1, z1)
-    g_end(4)
+    g_first(0)
+    swap_finish(1)
+    g_second(0)
     g_end(0)
-    g_end(1)
     for c in q_copies:
         c.wait_recv()
-    swap_finish(1)
 
     key_lane = lax.broadcasted_iota(jnp.int32, (1, 2 * CHUNK), 1)
     key_in = lax.rem(key_lane, CHUNK)
@@ -460,8 +431,12 @@
     ones = jnp.ones((2 * CHUNK, 128), BF16)
 
     def chunk_of(part, b, kv, ch):
-        rows = pl.ds(pl.multiple_of(lax.rem(ch, 2) * CHUNK, CHUNK), CHUNK)
-        return kvall[part, b, kv, lax.div(ch, 2), rows, :]
+        groups = pl.ds(pl.multiple_of(lax.rem(ch, 2) * 8, 8), 8)
+        return kvall[part, groups, rows_of(b, kv, lax.div(ch, 2)), :].reshape(CHUNK, 128)
+
+    def ques_block(kv):
+        first = 8 * TOK + kv * 16
+        return kvall[0, :, first:first + 16, :].reshape(256, 128)
 
     def transpose_keys(part):
         @pl.loop(0, 4)
@@ -535,8 +510,8 @@
 
     def ques_pass(part):
         closing = (
-            part == 0, lambda: jnp.transpose(kvq[0]),
-            lambda: jnp.concatenate([kvq[1], ones[0:256]], axis=1), ques_mask,
+            part == 0, lambda: jnp.transpose(ques_block(0)),
+            lambda: jnp.concatenate([ques_block(1), ones[0:256]], axis=1), ques_mask,
         )
         attend(
             1, 2 * QROWS, lambda b: jnp.concatenate([qall[j, ROWS:, :] for j in range(2)], axis=0),
@@ -581,13 +556,11 @@
         def _(t):
             @pl.when((part == 0) & (t == 0))
             def _():
-                g_first(2)
-                g_first(3)
+                g_first(1)
 
             @pl.when((part == 0) & (t == 1))
             def _():
-                g_second(2)
-                g_second(3)
+                g_second(1)
 
             c = lax.rem(z_lo + 1 + t, 2)
             rec_pass(part, c)
@@ -603,8 +576,7 @@
 
         @pl.when(part == 0)
         def _():
-            g_end(2)
-            g_end(3)
+            g_end(1)
 
     orecv[z_lo] = osend[z_lo]
     lrecv[z_lo] = lsend[z_lo]
@@ -636,7 +608,7 @@
 
     for c in plain0 + plain1 + merged1 + z0 + z1 + q_copies + out_copies:
         c.wait_send()
-    for fam in range(5):
+    for fam in range(2):
         g_sent(fam)
     for part in range(NP):
         swap_copy(part).wait_send()
@@ -664,17 +636,16 @@
             smem((512,), i32), smem((512,), i32), smem((32,), i32), smem((1,), i32),
             v((1, 128), i32), v((1, 128), F32), v((RECP, HEADS * HD), BF16),
             v((2, RECP, 256), BF16), v((QDEV, HEADS * HD), BF16), v((2, QDEV, 128), BF16),
-            v((3, 2, 2, 2, TOK, 256), BF16), v((3, 2, 2, 2, TOK, 256), BF16),
-            v((2, 2, 2, TOK, 256), BF16), v((2, 2, 2, TOK, 256), BF16),
-            v((2, 2, 2, TOK, 256), BF16), v((2, 2, 2, TOK, 256), BF16),
+            v((4, 2, 4, 128, 256), BF16),
+            v((NP, 2, 2, 4, TOK, 256), BF16),
+            v((NP, 2, 2, 2, TOK, 256), BF16),
             v((NP, 2, 2, 2, TOK, 256), BF16),
             v((NP, 2, 4, 2, TOK, 128), BF16),
             v((8, 2, TOK, 128), BF16), v((8, 2, TOK, 128), BF16),
             v((NP, 4, 2, TOK, 128), F32),
             v((NP, 4, TOK, 128), F32),
             v((NP, 4, 2, TOK, 256), F32),
-            v((NP, 2, 2, 2, 16 * TOK, 128), BF16),
-            v((2, 256, 128), BF16),
+            v((NP, 16, 8 * TOK + 32, 128), BF16),
             v((2, ROWS + QROWS, 128), BF16),
             v((2, 8, 128), F32),
             v((4, 128, 2 * CHUNK), BF16),
@@ -684,14 +655,14 @@
             v((2, 8, 128), F32),
             v((2, 8, 128), F32),
             dma((12,)),
-            dma((NP, 2, 4)),
-            dma((NP, 6, 2)), dma((NP, 6, 2)),
+            dma((2, 4)),
+            dma((NP, 6)), dma((NP, 6)),
             dma((NP, 7)), dma((NP, 7)),
             dma((NP,)), dma((NP,)),
             dma((2,)), dma((2,)),
-            dma((5, 4)), dma((5, 4)),
-            dma((5, 4)), dma((5, 4)),
-            dma((5, 8)), dma((5, 8)),
+            dma((NP, 4)), dma((NP, 4)),
+            dma((NP, 4)), dma((NP, 4)),
+            dma((NP, 8)), dma((NP, 8)),
             dma((2,)), dma((2,)),
         ],
         compiler_params=pltpu.CompilerParams(

time: 96.6 us -> 101 us (1.046)
  Pallas kernels: 91.4 us -> 96.4 us
    pallas_call x1, Pallas kernels: 91.4 us -> 96.4 us  [on_device(): pl.pallas_call(kernel, out_shape=(jax.ShapeDtypeStruct((RECP, HEADS * HD)...]
where the time goes in v6:
time: 101 us; the launch traced here: 99.9 us
  Pallas kernels  96.4 us (95%)
  local copies, waits for them, and re-layouts  2.23 us (2%)
  between operations  1.3 us (1%)
    pallas_call x1, Pallas kernels, on_device(): pl.pallas_call(kernel, out_shape=(jax.ShapeDtypeStruct((RECP, HEADS * HD)...  96.4 us
    unnamed x4, local copies, waits for them, and re-layouts  2.23 us

profile of v6, /device:TPU:56, one launch (start us, length us, event | category | flops | bytes accessed | tf_op | source)
XLA Modules:
  0.0 99.9 jit_solution(9153823907186571302)
XLA Ops:
  1.3 96.4 %blend_attend.1 = (bf16[128,768]{1,0:T(8,128)(2,1)}, bf16[16,768]{1,0:T(8,128)(2,1)}) custom-call(s32[512]{0:T(512)} %pos_off_h.1, s32[512]{0:T(512)} %owner_map_h.1, s32[32]{0:T(128)} %pids_h.1, s32[1]{0:T(128)S(6)} %copy.18.rec_count_h, s32[1,128]{1,0:T(1,128)} %rec_index_h.1, f32[1,128]{1,0:T(1,128)} %constant.2.clone.freq_h, bf16[128,768]{1,0:T(8,128)(2,1)} %fresh_q_h.1, ...), custom_call_target="tpu_custom_call" | custom-call | flops 8000000000 | bytes 4000000 | tf_op jit(solution)/shard_map/blend_attend/pallas_call | solution.py:627
  97.7 0.0 copy-start
  97.7 1.6 %copy.19 = bf16[128,768]{1,0:T(8,128)(2,1)} copy(bf16[128,768]{1,0:T(8,128)(2,1)} %get-tuple-element.4) | data formatting | bytes 393216
  99.3 0.0 copy-done
  99.3 0.6 copy.20
Async XLA Ops:
  97.7 1.6 %copy-start = (bf16[16,768]{1,0:T(8,128)(2,1)S(1)}, bf16[16,768]{1,0:T(8,128)(2,1)}, u32[]{:S(2)}) copy-start(bf16[16,768]{1,0:T(8,128)(2,1)} %get-tuple-element.5) | copy-start | bytes 73732

commit v7 on v5

--- a/solution.py
+++ b/solution.py
@@ -85,7 +85,7 @@
     fresh_v_h, ques_q_h, ques_k_h, ques_v_h, k_store, v_store,
     rec_out, ques_out,
     pos_off, owner_map, pids, rec_count, rec_index, freq_ref, fresh_q, fresh_kv, ques_q, ques_kv,
-    xfin, mbuf, msend, zsend, zin, tab, keep, repl, kvall, kvq,
+    stage, xfin, mbuf, msend, zsend, zin, tab, keep, repl, kvall,
     qall, qpos, kt, mst, ast,
     osend, orecv, lsend, lrecv,
     isem, lsem, xs, xr, zs, zr, bs, br, qs, qr, ps, pr, ns, nr, cs, cr, os_, or_,
@@ -147,55 +147,38 @@
     for c in moves:
         c.start()
 
-    stores = (k_store, v_store)
+    staged = []
+    for kv, st in enumerate((k_store, v_store)):
+        for t in range(4):
+            c = pltpu.make_async_copy(st.at[:, :, t * 256:(t + 1) * 256], stage.at[t, kv], lsem.at[kv, t])
+            c.start()
+            staged.append(c)
     top = pl.ds(0, 2)
     low = pl.ds(2, 2)
 
     def toks(part):
         return pl.ds(part * TOK, TOK)
 
-    def x_local(part):
-        copies = []
-        for kv in range(2):
-            st = stores[kv]
-            for j, (src, dst) in enumerate((
-                (st.at[top, toks(part), cols(x + 1)], mbuf[part][0].at[0, kv]),
-                (st.at[low, toks(part), cols(x + 3)], mbuf[part][1].at[0, kv]),
-                (st.at[top, toks(part), cols(x)], xfin[part].at[0, kv, 0]),
-                (st.at[low, toks(part), cols(x)], xfin[part].at[0, kv, 1]),
-            )):
-                c = pltpu.make_async_copy(src, dst, lsem.at[part, kv, j])
-                c.start()
-                copies.append(c)
-        return copies
-
-    loc = [x_local(part) for part in range(NP)]
+    for c in staged:
+        c.wait()
     pl.semaphore_wait(barrier, len(peers))
 
     def x_relay(part):
-        copies = []
-        for kv in range(2):
-            st = stores[kv]
-            copies += [
-                rcopy(st.at[top, toks(part), cols(x + 2)], mbuf[part][0].at[1, kv],
-                      xs.at[part, 0, kv], xr.at[part, 0, kv], x_up),
-                rcopy(st.at[low, toks(part), cols(x + 2)], mbuf[part][1].at[1, kv],
-                      xs.at[part, 1, kv], xr.at[part, 1, kv], x_dn),
-            ]
+        far = lax.rem(x + 2, 4)
+        copies = [
+            rcopy(stage.at[far, :, top, toks(part)], mbuf.at[part, 0], xs.at[part, 0], xr.at[part, 0], x_up),
+            rcopy(stage.at[far, :, low, toks(part)], mbuf.at[part, 1], xs.at[part, 1], xr.at[part, 1], x_dn),
+        ]
         for c in copies:
             c.start()
         return copies
 
     def x_plain(part):
-        copies = []
-        for kv in range(2):
-            st = stores[kv]
-            copies += [
-                rcopy(st.at[low, toks(part), cols(x + 1)], xfin[part].at[1, kv, 1],
-                      xs.at[part, 2, kv], xr.at[part, 2, kv], x_up),
-                rcopy(st.at[top, toks(part), cols(x + 3)], xfin[part].at[2, kv, 0],
-                      xs.at[part, 3, kv], xr.at[part, 3, kv], x_dn),
-            ]
+        up, dn = lax.rem(x + 1, 4), lax.rem(x + 3, 4)
+        copies = [
+            rcopy(stage.at[up, :, low, toks(part)], xfin.at[part, 0, :, low], xs.at[part, 2], xr.at[part, 2], x_up),
+            rcopy(stage.at[dn, :, top, toks(part)], xfin.at[part, 1, :, top], xs.at[part, 3], xr.at[part, 3], x_dn),
+        ]
         for c in copies:
             c.start()
         return copies
@@ -203,33 +186,33 @@
     def x_merge(part, relay, owner_x):
         copies = []
         for d in range(2):
-            for kv in range(2):
-                loc[part][kv * 4 + d].wait()
-                relay[kv * 2 + d].wait_recv()
-            near = lax.rem(x + (3 if d == 0 else 1), 4)
-            pick = jnp.where(owner_x == near, 1, 0)
-            msend[part, d] = mbuf[part][d][pick]
-            c = rcopy(msend.at[part, d], xfin[part].at[1 + d, :, d],
-                      xs.at[part, 4 + d, 0], xr.at[part, 4 + d, 0], x_up if d == 0 else x_dn)
+            half = (top, low)[d]
+            relay[d].wait_recv()
+            target = lax.rem(x + (1 if d == 0 else 3), 4)
+            source = lax.rem(x + (3 if d == 0 else 1), 4)
+            mine = stage[target, :, half, toks(part), :]
+            msend[part, d] = jnp.where(owner_x == source, mbuf[part, d], mine)
+            c = rcopy(msend.at[part, d], xfin.at[part, d, :, half], xs.at[part, 4 + d], xr.at[part, 4 + d],
+                      x_up if d == 0 else x_dn)
             c.start()
             copies.append(c)
         return copies
 
     def x_finish(part, plain, merged, owner_x):
         at_tok = slice(part * TOK, (part + 1) * TOK)
-        for kv in range(2):
-            loc[part][kv * 4 + 2].wait()
-            loc[part][kv * 4 + 3].wait()
         for c in plain + merged:
             c.wait_recv()
         is_own = owner_x == x
-        idx_a = jnp.where(is_own, 0, jnp.where(owner_x == lax.rem(x + 1, 4), 2, 1))
-        idx_b = jnp.where(is_own, 0, jnp.where(owner_x == lax.rem(x + 3, 4), 1, 2))
+        from_up = owner_x == lax.rem(x + 1, 4)
+        from_dn = owner_x == lax.rem(x + 3, 4)
         for kv in range(2):
             for quarter in range(4):
-                half = quarter // 2
-                idx = idx_a if half == 0 else idx_b
-                data = xfin[part][idx, kv, half, quarter % 2].astype(F32)
+                sides = [xfin[part, side, kv, quarter] for side in range(2)]
+                if quarter < 2:
+                    data = jnp.where(from_up, sides[1], sides[0])
+                else:
+                    data = jnp.where(from_dn, sides[0], sides[1])
+                data = jnp.where(is_own, stage[x, kv, quarter, toks(part), :], data).astype(F32)
                 for hh in range(2):
                     lanes = slice(hh * 128, (hh + 1) * 128)
                     piece = data[:, lanes]
@@ -251,11 +234,14 @@
         zin[part][0] = zsend[part, zh, z4]
         return copies
 
-    def g_rows(gg):
-        return pl.ds(pl.multiple_of(gg * TOK, TOK), TOK)
+    def rows_of(b, kv, c):
+        return pl.ds(pl.multiple_of(((b * 2 + kv) * 2 + c) * TOK, TOK), TOK)
+
+    def half_of(b):
+        return pl.ds(pl.multiple_of(b * 4 * TOK, 4 * TOK), 4 * TOK)
 
     def swap_copy(part):
-        piece = kvall.at[part, b1, :, :, g_rows(g), :]
+        piece = kvall.at[part, g, half_of(b1), :]
         return rcopy(piece, piece, bs.at[part], br.at[part], other_b)
 
     def z_finish(part, copies):
@@ -264,20 +250,20 @@
         for c in range(2):
             owner_z = lax.rem(lax.div(owner_map[pids[c * 16 + g]], 32), 4)
             idx = lax.rem(zc + 8 - (2 * owner_z + c), 8)
-            kvall[part, b1, 0, c, g_rows(g), :] = zin[part][idx, 0]
-            kvall[part, b1, 1, c, g_rows(g), :] = zin[part][idx, 1]
+            for kv in range(2):
+                kvall[part, g, rows_of(b1, kv, c), :] = zin[part][idx, kv]
         swap_copy(part).start()
         g_start(part, 0)
 
     def swap_finish(part):
-        piece = kvall.at[part, 1 - b1, :, :, g_rows(g), :]
+        piece = kvall.at[part, g, half_of(1 - b1), :]
         rcopy(piece, piece, bs.at[part], br.at[part], other_b).wait_recv()
         g_start(part, 1)
 
     def gather_slices(part, o, gg):
         if o < 2:
-            return kvall.at[part, b1 if o == 0 else 1 - b1, :, :, g_rows(gg), :]
-        return kvq.at[:, pl.ds(pl.multiple_of(gg * 16, 16), 16), :]
+            return kvall.at[part, gg, half_of(b1 if o == 0 else 1 - b1), :]
+        return kvall.at[0, gg, pl.ds(8 * TOK, 32), :]
 
     def reach(o):
         return (4, 3) if o % 2 == 0 else (3, 4)
@@ -420,9 +406,8 @@
         c.start()
         q_copies.append(c)
 
-    my_rows = pl.ds(pl.multiple_of(g * 16, 16), 16)
-    kvq[0, my_rows, :] = turn(ques_kv[0].astype(F32), c_q, s_q).astype(BF16)
-    kvq[1, my_rows, :] = ques_kv[1]
+    kvall[0, g, 8 * TOK:8 * TOK + 16, :] = turn(ques_kv[0].astype(F32), c_q, s_q).astype(BF16)
+    kvall[0, g, 8 * TOK + 16:8 * TOK + 32, :] = ques_kv[1]
     g_start(0, 2)
     after(merged0)
     relay1 = x_relay(1)
@@ -476,7 +461,11 @@
     ones = jnp.ones((2 * CHUNK, 128), BF16)
 
     def chunk_of(part, b, kv, ch):
-        return kvall[part, b, kv, ch]
+        return kvall[part, :, rows_of(b, kv, ch), :].reshape(CHUNK, 128)
+
+    def ques_block(kv):
+        first = 8 * TOK + kv * 16
+        return kvall[0, :, first:first + 16, :].reshape(256, 128)
 
     def transpose_keys(part):
         for ch in range(2):
@@ -549,8 +538,8 @@
 
     def ques_pass(part):
         closing = (
-            part == 0, lambda: jnp.transpose(kvq[0]),
-            lambda: jnp.concatenate([kvq[1], ones[0:256]], axis=1), ques_mask,
+            part == 0, lambda: jnp.transpose(ques_block(0)),
+            lambda: jnp.concatenate([ques_block(1), ones[0:256]], axis=1), ques_mask,
         )
         attend(
             1, 2 * QROWS, lambda b: jnp.concatenate([qall[j, ROWS:, :] for j in range(2)], axis=0),
@@ -683,16 +672,16 @@
             smem((512,), i32), smem((512,), i32), smem((32,), i32), smem((1,), i32),
             v((1, 128), i32), v((1, 128), F32), v((RECP, HEADS * HD), BF16),
             v((2, RECP, 256), BF16), v((QDEV, HEADS * HD), BF16), v((2, QDEV, 128), BF16),
-            (v((3, 2, 2, 2, TOK, 256), BF16),) * NP,
-            ((v((2, 2, 2, TOK, 256), BF16),) * 2,) * NP,
+            v((4, 2, 4, 128, 256), BF16),
+            v((NP, 2, 2, 4, TOK, 256), BF16),
+            v((NP, 2, 2, 2, TOK, 256), BF16),
             v((NP, 2, 2, 2, TOK, 256), BF16),
             v((NP, 2, 4, 2, TOK, 128), BF16),
             (v((8, 2, TOK, 128), BF16),) * NP,
             v((4, 2, 128, 128), F32),
             v((4, 128, 128), F32),
             v((4, 2, 128, 256), F32),
-            v((NP, 2, 2, 2, 16 * TOK, 128), BF16),
-            v((2, 256, 128), BF16),
+            v((NP, 16, 8 * TOK + 32, 128), BF16),
             v((2, ROWS + QROWS, 128), BF16),
             v((2, 8, 128), F32),
             v((2, 128, 2 * CHUNK), BF16),
@@ -702,8 +691,8 @@
             v((2, 8, 128), F32),
             v((2, 8, 128), F32),
             dma((12,)),
-            dma((NP, 2, 4)),
-            dma((NP, 6, 2)), dma((NP, 6, 2)),
+            dma((2, 4)),
+            dma((NP, 6)), dma((NP, 6)),
             dma((NP, 7)), dma((NP, 7)),
             dma((NP,)), dma((NP,)),
             dma((2,)), dma((2,)),

time: 99.6 us -> 98.2 us (0.986)
  Pallas kernels: 94.4 us -> 93.2 us
    pallas_call x1, Pallas kernels: 94.4 us -> 93.2 us  [on_device(): pl.pallas_call(kernel, out_shape=(jax.ShapeDtypeStruct((RECP, HEADS * HD)...]
where the time goes in v7:
time: 98.2 us; the launch traced here: 96.7 us
  Pallas kernels  93.2 us (95%)
  local copies, waits for them, and re-layouts  2.23 us (2%)
  between operations  1.3 us (1%)
    pallas_call x1, Pallas kernels, on_device(): pl.pallas_call(kernel, out_shape=(jax.ShapeDtypeStruct((RECP, HEADS * HD)...  93.2 us
    unnamed x4, local copies, waits for them, and re-layouts  2.23 us

profile of v7, /device:TPU:56, one launch (start us, length us, event | category | flops | bytes accessed | tf_op | source)
XLA Modules:
  0.0 96.7 jit_solution(9109622409534000171)
XLA Ops:
  1.3 93.2 %blend_attend.1 = (bf16[128,768]{1,0:T(8,128)(2,1)}, bf16[16,768]{1,0:T(8,128)(2,1)}) custom-call(s32[512]{0:T(512)} %pos_off_h.1, s32[512]{0:T(512)} %owner_map_h.1, s32[32]{0:T(128)} %pids_h.1, s32[1]{0:T(128)S(6)} %copy.18.rec_count_h, s32[1,128]{1,0:T(1,128)} %rec_index_h.1, f32[1,128]{1,0:T(1,128)} %constant.2.clone.freq_h, bf16[128,768]{1,0:T(8,128)(2,1)} %fresh_q_h.1, ...), custom_call_target="tpu_custom_call" | custom-call | flops 8000000000 | bytes 4000000 | tf_op jit(solution)/shard_map/blend_attend/pallas_call | solution.py:663
  94.5 0.0 copy-start
  94.5 1.6 %copy.19 = bf16[128,768]{1,0:T(8,128)(2,1)} copy(bf16[128,768]{1,0:T(8,128)(2,1)} %get-tuple-element.4) | data formatting | bytes 393216
  96.1 0.0 copy-done
  96.1 0.6 copy.20
Async XLA Ops:
  94.5 1.6 %copy-start = (bf16[16,768]{1,0:T(8,128)(2,1)S(1)}, bf16[16,768]{1,0:T(8,128)(2,1)}, u32[]{:S(2)}) copy-start(bf16[16,768]{1,0:T(8,128)(2,1)} %get-tuple-element.5) | copy-start | bytes 73732

commit v8 on v7

--- a/solution.py
+++ b/solution.py
@@ -337,7 +337,8 @@
         for dy, hop in twin_hops(o):
             g_copy(part, o, dy, "twin", hop).wait_send()
 
-    relay0 = x_relay(0)
+    relays = [x_relay(part) for part in range(NP)]
+    plain0 = x_plain(0)
     for c in moves:
         c.wait()
     slot = owner_map[pids[blk]]
@@ -373,13 +374,9 @@
         tab[quarter, 1] = s_t * stay
 
 
-    def after(copies):
-        for c in copies:
-            c.wait_send()
-
-    after(relay0)
-    plain0 = x_plain(0)
-    merged0 = x_merge(0, relay0, owner_x)
+    merged0 = x_merge(0, relays[0], owner_x)
+    plain1 = x_plain(1)
+    merged1 = x_merge(1, relays[1], owner_x)
 
     rec_pos_row = rec_row + (blk * PT).astype(F32)
     rec_pos = to_col(rec_pos_row, 128)
@@ -409,31 +406,20 @@
     kvall[0, g, 8 * TOK:8 * TOK + 16, :] = turn(ques_kv[0].astype(F32), c_q, s_q).astype(BF16)
     kvall[0, g, 8 * TOK + 16:8 * TOK + 32, :] = ques_kv[1]
     g_start(0, 2)
-    after(merged0)
-    relay1 = x_relay(1)
     z0 = x_finish(0, plain0, merged0, owner_x)
-    after(relay1)
-    plain1 = x_plain(1)
-    merged1 = x_merge(1, relay1, owner_x)
-    after(merged1)
-    relay2 = x_relay(2)
+    plain2 = x_plain(2)
+    merged2 = x_merge(2, relays[2], owner_x)
     z1 = x_finish(1, plain1, merged1, owner_x)
-    after(relay2)
-    plain2 = x_plain(2)
-    merged2 = x_merge(2, relay2, owner_x)
+    plain3 = x_plain(3)
+    merged3 = x_merge(3, relays[3], owner_x)
+    z2 = x_finish(2, plain2, merged2, owner_x)
     g_first(0, 2)
     z_finish(0, z0)
-    after(merged2)
-    relay3 = x_relay(3)
-    z2 = x_finish(2, plain2, merged2, owner_x)
-    after(relay3)
-    plain3 = x_plain(3)
-    merged3 = x_merge(3, relay3, owner_x)
+    z3 = x_finish(3, plain3, merged3, owner_x)
     swap_finish(0)
     z_finish(1, z1)
     g_first(0, 0)
     g_second(0, 2)
-    z3 = x_finish(3, plain3, merged3, owner_x)
     g_first(0, 1)
     swap_finish(1)
     g_first(1, 0)
@@ -639,6 +625,8 @@
     for hh in range(HEADS):
         ques_out[:, hh * 128:(hh + 1) * 128] = o[hh * 16:(hh + 1) * 16].astype(BF16)
 
+    for c in sum(relays, []) + merged0 + merged1 + merged2:
+        c.wait_send()
     for c in plain0 + plain1 + plain2 + plain3 + merged3 + z0 + z1 + z2 + z3 + q_copies + out_copies:
         c.wait_send()
     g_sent(0, 2)

time: 98.2 us -> 103 us (1.049)
  the two profiles are of different devices: /device:TPU:56 before, /device:TPU:64 now
where the time goes in v8:
time: 103 us
  Pallas kernels  99.7 us (97%)
  local copies, waits for them, and re-layouts  2.23 us (2%)
  between operations  1.3 us (1%)
    pallas_call x1, Pallas kernels, on_device(): pl.pallas_call(kernel, out_shape=(jax.ShapeDtypeStruct((RECP, HEADS * HD)...  99.7 us
    unnamed x4, local copies, waits for them, and re-layouts  2.23 us

profile of v8, /device:TPU:64, one launch (start us, length us, event | category | flops | bytes accessed | tf_op | source)
XLA Modules:
  0.0 103.2 jit_solution(1351245655624427032)
XLA Ops:
  1.3 99.7 %blend_attend.1 = (bf16[128,768]{1,0:T(8,128)(2,1)}, bf16[16,768]{1,0:T(8,128)(2,1)}) custom-call(s32[512]{0:T(512)} %pos_off_h.1, s32[512]{0:T(512)} %owner_map_h.1, s32[32]{0:T(128)} %pids_h.1, s32[1]{0:T(128)S(6)} %copy.18.rec_count_h, s32[1,128]{1,0:T(1,128)} %rec_index_h.1, f32[1,128]{1,0:T(1,128)} %constant.2.clone.freq_h, bf16[128,768]{1,0:T(8,128)(2,1)} %fresh_q_h.1, ...), custom_call_target="tpu_custom_call" | custom-call | flops 8000000000 | bytes 4000000 | tf_op jit(solution)/shard_map/blend_attend/pallas_call | solution.py:651
  101.0 0.0 copy-start
  101.0 1.6 %copy.19 = bf16[128,768]{1,0:T(8,128)(2,1)} copy(bf16[128,768]{1,0:T(8,128)(2,1)} %get-tuple-element.4) | data formatting | bytes 393216
  102.6 0.0 copy-done
  102.6 0.6 copy.20
Async XLA Ops:
  101.0 1.6 %copy-start = (bf16[16,768]{1,0:T(8,128)(2,1)S(1)}, bf16[16,768]{1,0:T(8,128)(2,1)}, u32[]{:S(2)}) copy-start(bf16[16,768]{1,0:T(8,128)(2,1)} %get-tuple-element.5) | copy-start | bytes 73732

commit v9 on v4

--- a/solution.py
+++ b/solution.py
@@ -440,18 +440,19 @@
     g_first(4)
     g_second(4)
     z_finish(0, z0)
+    z1 = x_finish(1, plain1, merged1, owner_x, None)
     swap_finish(0)
-    z1 = x_finish(1, plain1, merged1, owner_x, None)
-    for step in (g_first, g_second):
-        step(0)
-        step(1)
+    g_first(0)
     z_finish(1, z1)
+    g_first(1)
+    swap_finish(1)
+    g_second(0)
+    g_second(1)
     g_end(4)
     g_end(0)
     g_end(1)
     for c in q_copies:
         c.wait_recv()
-    swap_finish(1)
 
     key_lane = lax.broadcasted_iota(jnp.int32, (1, 2 * CHUNK), 1)
     key_in = lax.rem(key_lane, CHUNK)

time: 96.6 us -> 93.4 us (0.967)
  Pallas kernels: 91.4 us -> 89.2 us
    pallas_call x1, Pallas kernels: 91.4 us -> 89.2 us  [on_device(): pl.pallas_call(kernel, out_shape=(jax.ShapeDtypeStruct((RECP, HEADS * HD)...]
where the time goes in v9:
time: 93.4 us; the launch traced here: 92.7 us
  Pallas kernels  89.2 us (96%)
  local copies, waits for them, and re-layouts  2.23 us (2%)
  between operations  1.3 us (1%)
    pallas_call x1, Pallas kernels, on_device(): pl.pallas_call(kernel, out_shape=(jax.ShapeDtypeStruct((RECP, HEADS * HD)...  89.2 us
    unnamed x4, local copies, waits for them, and re-layouts  2.23 us

profile of v9, /device:TPU:56, one launch (start us, length us, event | category | flops | bytes accessed | tf_op | source)
XLA Modules:
  0.0 92.7 jit_solution(13826576098945393671)
XLA Ops:
  1.3 89.2 %blend_attend.1 = (bf16[128,768]{1,0:T(8,128)(2,1)}, bf16[16,768]{1,0:T(8,128)(2,1)}) custom-call(s32[512]{0:T(512)} %pos_off_h.1, s32[512]{0:T(512)} %owner_map_h.1, s32[32]{0:T(128)} %pids_h.1, s32[1]{0:T(128)S(6)} %copy.18.rec_count_h, s32[1,128]{1,0:T(1,128)} %rec_index_h.1, f32[1,128]{1,0:T(1,128)} %constant.2.clone.freq_h, bf16[128,768]{1,0:T(8,128)(2,1)} %fresh_q_h.1, ...), custom_call_target="tpu_custom_call" | custom-call | flops 8000000000 | bytes 4000000 | tf_op jit(solution)/shard_map/blend_attend/pallas_call | solution.py:656
  90.5 0.0 copy-start
  90.5 1.6 %copy.19 = bf16[128,768]{1,0:T(8,128)(2,1)} copy(bf16[128,768]{1,0:T(8,128)(2,1)} %get-tuple-element.4) | data formatting | bytes 393216
  92.1 0.0 copy-done
  92.1 0.6 copy.20
Async XLA Ops:
  90.5 1.6 %copy-start = (bf16[16,768]{1,0:T(8,128)(2,1)S(1)}, bf16[16,768]{1,0:T(8,128)(2,1)}, u32[]{:S(2)}) copy-start(bf16[16,768]{1,0:T(8,128)(2,1)} %get-tuple-element.5) | copy-start | bytes 73732
